TPU v7x, 32 devices: a whole 2x2x4 slice. The times are simulated.
32 devices in a mesh: section: 2 (over y), row: 4 (over x, core), col: 4 (over z).
Axes of the slice: x: 2, y: 2, z: 4, core: 2. Of those that a mesh axis runs over, the one named last changes fastest.
Arguments:
- x_down: bfloat16 [2, 1024, 8192], P('section', 'row', 'col'), may hold values from -30 to 30
- gain_down: float32 [2, 8192], P('section', 'col'), may hold values from 0.1 to 1.9
- wq_down: bfloat16 [2, 8192, 4096], P('section', 'col', 'row'), may hold values from -2 to 2
- wk_down: bfloat16 [2, 8192, 512], P('section', 'col', 'row'), may hold values from -1 to 1
- wv_down: bfloat16 [2, 8192, 512], P('section', 'col', 'row'), may hold values from -0.0625 to 0.0625
- wo_down: bfloat16 [2, 4096, 8192], P('section', 'row', 'col'), may hold values from -0.09375 to 0.09375
- x_up: bfloat16 [2, 1024, 8192], P('section', 'row', 'col'), may hold values from -30 to 30
- gain_up: float32 [2, 8192], P('section', 'col'), may hold values from 0.1 to 1.9
- wq_up: bfloat16 [2, 8192, 4096], P('section', 'col', 'row'), may hold values from -2 to 2
- wk_up: bfloat16 [2, 8192, 512], P('section', 'col', 'row'), may hold values from -1 to 1
- wv_up: bfloat16 [2, 8192, 512], P('section', 'col', 'row'), may hold values from -0.0625 to 0.0625
- wo_up: bfloat16 [2, 4096, 8192], P('section', 'row', 'col'), may hold values from -0.09375 to 0.09375
Outputs:
- next_down: bfloat16 [2, 1024, 8192], P('section', 'row', 'col')
- next_up: bfloat16 [2, 1024, 8192], P('section', 'row', 'col')
All inputs are finite; a program needn't handle non-finite values.
Results may differ from a plain program's by a relative error of at most 0.0055.
Values may be sent and summed in bfloat16 or wider, within the bound.
No kernel may reach another device: no remote copies, remote signals or barrier semaphores. Data moves between devices by JAX's collectives and lax.ppermute only.
A program may use at most 128 MiB of HBM per device.

v0:
```python
import functools

import jax
import jax.numpy as jnp
from jax import lax
from jax.experimental import pallas as pl
from jax.experimental.pallas import tpu as pltpu
from jax.sharding import PartitionSpec as P

HD = 128
EPSILON = 1e-05
HIDDEN = -1e30
LOG2E = 1.4426950408889634
BF16 = jnp.bfloat16
F32 = jnp.float32


def swapped(value, axis, bit):
    return lax.ppermute(value, axis, [(i, i ^ (1 << bit)) for i in range(lax.axis_size(axis))])


def crossed(value, axis, bits):
    return lax.ppermute(value, axis, [(i, i ^ bits) for i in range(lax.axis_size(axis))])


def from_behind(value, axis, steps):
    count = lax.axis_size(axis)
    return lax.ppermute(value, axis, [(i, (i + steps) % count) for i in range(count)])


def bits_of(axis):
    return lax.axis_size(axis).bit_length() - 1


def my_bit(axis, bit):
    return (lax.axis_index(axis) >> bit) & 1


def pick(value, index, dim):
    return lax.dynamic_index_in_dim(value, index, dim, keepdims=False)


def tie(value, *deps):
    return lax.optimization_barrier((value, deps))[0]


class Chain:
    def __init__(self):
        self.token = None

    def enter(self, *values):
        out = values if self.token is None else tie(values, self.token)
        return out[0] if len(values) == 1 else out

    def leave(self, array):
        self.token = array


def turn(value, cosine, sine):
    return value * cosine + pltpu.roll(value, HD // 2, 1) * sine


def rows_of(keeps, arrivals, inverse, columns):
    parts = [k[:, columns] + a[:, columns].astype(F32) for k, a in zip(keeps, arrivals)]
    return jnp.concatenate(parts, axis=0) * inverse[...]


def kv_kernel(qw, kvw, keep_a, keep_b, arr_a, arr_b, inverse, cosine, sine, out):
    for start in range(0, 2 * kvw, HD):
        columns = slice(qw + start, qw + start + HD)
        value = rows_of((keep_a, keep_b), (arr_a, arr_b), inverse, columns)
        if start < kvw:
            value = turn(value, cosine[...], sine[...])
        out[:, start : start + HD] = value.astype(BF16)


def attention_kernel(
    qw, kvw, count, keep_a, keep_b, arr_a, arr_b, inverse, cosine, sine, q_pos, k_pos, *rest
):
    pairs, (out, keys, values, bias) = rest[:count], rest[count:]
    rows = pairs[0].shape[0]
    for i, pair in enumerate(pairs):
        keys[i * rows : (i + 1) * rows] = pair[:, :kvw]
        values[i * rows : (i + 1) * rows] = pair[:, kvw:]
    bias[...] = jnp.where(q_pos[...] >= k_pos[...], 0.0, HIDDEN)
    group = (qw // HD) // (kvw // HD)
    for head in range(qw // HD):
        columns = slice(head * HD, (head + 1) * HD)
        kv_columns = slice(head // group * HD, (head // group + 1) * HD)
        query = rows_of((keep_a, keep_b), (arr_a, arr_b), inverse, columns)
        query = turn(query, cosine[...], sine[...]).astype(BF16)
        scores = lax.dot_general(
            query, keys[:, kv_columns], (((1,), (1,)), ((), ())), preferred_element_type=F32
        )
        scores = scores + bias[...]
        top = jnp.max(scores, axis=1, keepdims=True)
        probs = jnp.exp2((scores - top) * (LOG2E / HD**0.5))
        total = jnp.sum(probs, axis=1, keepdims=True)
        mixed = jnp.dot(probs.astype(BF16), values[:, kv_columns], preferred_element_type=F32)
        out[:, columns] = (mixed / total).astype(BF16)


def gather(block, axis, after_far=None):
    blocks = {0: block}
    for bit in range(1, bits_of(axis)):
        for o in list(blocks):
            blocks[o | 1 << bit] = swapped(blocks[o], axis, bit)
    return blocks


class Cascade:
    def __init__(self, x, gain, wq, wk, wv, wo):
        self.x, self.gain, self.wo = x, gain, wo
        if wk.shape[1] < HD:
            other_k, other_v = swapped((wk, wv), "row", 0)
            even = lax.axis_index("row") % 2 == 0
            wk = jnp.where(even, jnp.concatenate([wk, other_k], 1), jnp.concatenate([other_k, wk], 1))
            wv = jnp.where(even, jnp.concatenate([wv, other_v], 1), jnp.concatenate([other_v, wv], 1))
        self.qw, self.kvw = wq.shape[1], wk.shape[1]
        self.w = jnp.concatenate([wq, wk, wv], axis=1)
        self.n_row, self.n_col = lax.axis_size("row"), lax.axis_size("col")
        self.sub = x.shape[0] // self.n_col
        self.keep, self.arrived = [], []
        self.first, self.second = [None, None], [None, None]

    def halves(self, block_list):
        low = my_bit("col", 0)
        blocks = jnp.stack(block_list).reshape(len(block_list), self.n_col // 2, 2, self.sub, -1)
        return pick(blocks, 1 - low, 2), pick(blocks, low, 2)

    def project(self, half):
        scaled = (half.astype(F32) * self.gain).astype(BF16)
        rows = scaled.reshape(-1, scaled.shape[-1])
        out = jnp.dot(rows, self.w, preferred_element_type=F32)
        return out.reshape(half.shape[:-1] + (-1,))

    def halve(self, total, arrived, bit):
        mine = my_bit("col", bit)
        shape = (total.shape[0], -1, 2) + total.shape[2:]
        total, arrived = total.reshape(shape), arrived.reshape(shape)

        def part(which):
            return pick(total, which, 2) + pick(arrived, which, 2).astype(F32)

        return part(mine), part(1 - mine).astype(BF16)

    def flat(self, value):
        return value.reshape(-1, value.shape[-1])

    def kernel_rows(self):
        return [self.flat(v) for v in self.keep] + [self.flat(v) for v in self.arrived]


def whole(body, out_shape, scratch=(), flops=0, exps=0, moved=0):
    return pl.pallas_call(
        body,
        out_shape=out_shape,
        scratch_shapes=list(scratch),
        compiler_params=pltpu.CompilerParams(vmem_limit_bytes=40 * 1024 * 1024),
        cost_estimate=pl.CostEstimate(flops=flops, transcendentals=exps, bytes_accessed=moved),
    )


def on_device(*arrays):
    arrays = [a[0] for a in arrays]
    half = len(arrays) // 2
    d, u = Cascade(*arrays[:half]), Cascade(*arrays[half:])
    n_row, n_col, sub = d.n_row, d.n_col, d.sub
    block = n_col * sub
    features = d.x.shape[1] * n_col
    rows = n_row * sub
    qw, kvw = d.qw, d.kvw
    z, r = lax.axis_index("col"), lax.axis_index("row")
    chain = Chain()

    order = [o for o in range(n_row) if o < 2] + [o for o in range(n_row) if o >= 2]
    starts = (r ^ jnp.array(order, jnp.int32)) * block
    offsets = jnp.arange(sub, dtype=jnp.int32)
    q_pos = (starts[:, None] + z * sub + offsets).astype(F32).reshape(rows, 1)
    owners = (z ^ jnp.arange(n_col, dtype=jnp.int32)) * sub
    k_pos = (owners[:, None, None] + starts[:, None] + offsets).astype(F32).reshape(1, -1)
    width = HD // 2
    inverse_freq = 10000.0 ** (-jnp.arange(width, dtype=F32) / width)
    angles = q_pos * inverse_freq
    cosine = jnp.concatenate([jnp.cos(angles)] * 2, axis=1)
    sine = jnp.sin(angles)
    sine = jnp.concatenate([-sine, sine], axis=1)

    d_blocks = gather(d.x, "row")
    d_blocks[1] = swapped(d.x, "row", 0)
    squares = jnp.stack([jnp.sum(jnp.square(c.x.astype(F32)), axis=1) for c in (d, u)])
    other = swapped(squares, "col", 0)

    def send_first(c, group, blocks_):
        send, kept = c.halves(chain.enter(*blocks_))
        product = c.project(send).astype(BF16)
        return product, kept

    def keep_first(c, kept, token):
        return c.project(tie(kept, token))

    product, kept = send_first(d, 0, [d_blocks[0], d_blocks[1]])
    d_arr_a = swapped(product, "col", 0)
    d_tot_a = keep_first(d, kept, product)
    chain.leave(d_tot_a)
    squares, other = chain.enter(squares, other)
    squares = squares + other
    for bit in range(1, bits_of("col")):
        squares = squares + swapped(squares, "col", bit)
    chain.leave(squares)
    u_near = swapped(chain.enter(u.x), "row", 0)

    far = [o for o in d_blocks if o >= 2]
    d_far = chain.enter(*[d_blocks[o] for o in far])
    d_far = list(d_far) if len(far) > 1 else [d_far]
    u_blocks = gather(tie(u.x, *d_far), "row")
    u_blocks[1] = u_near
    for o, value in zip(far, d_far):
        d_blocks[o] = value
        d_blocks[o | 1] = swapped(value, "row", 0)
    chain.leave(d_far[-1])
    sq = {0: squares}
    for bit in range(1, bits_of("row")):
        for o in list(sq):
            sq[o | 1 << bit] = swapped(tie(sq[o], *d_far), "row", bit)

    def second(c, total, arrived):
        total, arrived = chain.enter(total, arrived)
        kept, product = c.halve(total, arrived, 1)
        arrived = swapped(product, "col", 1)
        chain.leave(product)
        for bit in range(2, bits_of("col")):
            kept, product = c.halve(kept, arrived, bit)
            arrived = swapped(product, "col", bit)
        c.keep.append(kept)
        c.arrived.append(arrived)

    second(d, d_tot_a, d_arr_a)

    far_order = [o for o in order if o >= 2]
    product, kept = send_first(d, 1, [d_blocks[o] for o in far_order])
    d_arr_b = swapped(product, "col", 0)
    d_tot_b = keep_first(d, kept, product)
    chain.leave(d_tot_b)

    u_prod_a, kept = send_first(u, 0, [u_blocks[0], u_blocks[1]])
    u_tot_a = keep_first(u, kept, u_prod_a)
    chain.leave(u_tot_a)

    second(d, d_tot_b, d_arr_b)
    u_arr_a = swapped(tie(u_prod_a, chain.token), "col", 0)

    u_far = chain.enter(*[u_blocks[o] for o in far])
    u_far = list(u_far) if len(far) > 1 else [u_far]
    for o, value in zip(far, u_far):
        u_blocks[o] = value
        u_blocks[o | 1] = swapped(value, "row", 0)
    chain.leave(u_far[-1])
    for o in list(sq):
        sq[o | 1] = swapped(tie(sq[o], *u_far), "row", 0)
    u_prod_b, kept = send_first(u, 1, [u_blocks[o] for o in far_order])
    u_tot_b = keep_first(u, kept, u_prod_b)
    chain.leave(u_tot_b)

    sums = jnp.stack([sq[o] for o in order])
    sums = pick(sums.reshape(n_row, 2, n_col, sub), z, 2)
    inverse = lax.rsqrt(sums / features + EPSILON).transpose(1, 0, 2).reshape(2, rows, 1)

    def make_pairs(c, scale):
        inputs = chain.enter(*c.kernel_rows())
        pair = whole(
            functools.partial(kv_kernel, qw, kvw),
            jax.ShapeDtypeStruct((rows, 2 * kvw), BF16),
            moved=2 * rows * (qw + 2 * kvw) * 6,
        )(*inputs, scale, cosine, sine)
        chain.leave(pair)
        return inputs, [pair] + [crossed(pair, "col", o) for o in range(1, n_col)]

    def attend(c, inputs, scale, pairs):
        pairs = chain.enter(*pairs)
        keys = rows * n_col
        out = whole(
            functools.partial(attention_kernel, qw, kvw, n_col),
            jax.ShapeDtypeStruct((rows, qw), BF16),
            scratch=[pltpu.VMEM((keys, kvw), BF16), pltpu.VMEM((keys, kvw), BF16), pltpu.VMEM((rows, keys), F32)],
            flops=4 * rows * keys * qw,
            exps=rows * keys * qw // HD,
            moved=rows * qw * 8,
        )(*inputs, scale, cosine, sine, q_pos, k_pos, *pairs)
        chain.leave(out)
        return out

    d_inputs, d_pairs = make_pairs(d, inverse[0])
    second(u, u_tot_a, u_arr_a)
    u_arr_b = swapped(tie(u_prod_b, chain.token), "col", 0)
    d_att = attend(d, d_inputs, inverse[0], d_pairs)
    d_got = gather(d_att, "col")
    d_got[1] = swapped(d_att, "col", 0)
    second(u, u_tot_b, u_arr_b)

    order_rows = jnp.array(order)

    def out_first(c, pieces):
        pieces = chain.enter(*pieces)
        pieces = pieces if isinstance(pieces, (list, tuple)) else [pieces]
        shaped = jnp.stack([p.reshape(n_row // 2, 2, sub, qw) for p in pieces], axis=2)

        def dot(value):
            out = jnp.dot(value.reshape(-1, qw), c.wo, preferred_element_type=F32)
            return out.reshape(n_row // 2, -1, c.wo.shape[1])

        product = dot(shaped[:, 1]).astype(BF16)
        arrived = swapped(product, "row", 0)
        kept = dot(tie(shaped[:, 0], product))
        chain.leave(kept)
        return kept, arrived

    def out_second(kept, arrived):
        kept, arrived = chain.enter(kept, arrived)
        for bit in range(1, bits_of("row")):
            total = (kept + arrived.astype(F32)).reshape(-1, 2, *kept.shape[1:])
            product = total[:, 1].astype(BF16)
            kept, arrived = total[:, 0], swapped(product, "row", bit)
        chain.leave(product)
        return kept, arrived

    def out_third(c, kept, arrived, which, steps):
        kept, arrived = chain.enter(kept, arrived)
        residual = c.x.reshape(n_col, sub, -1)
        own = jnp.stack([pick(residual, z ^ o, 0) for o in which]).astype(F32)
        total = kept[0] + arrived[0].astype(F32)
        fresh = (own + total.reshape(own.shape)).astype(BF16)
        chain.leave(fresh)
        return from_behind(fresh, "section", steps)

    def finish(c, sent_p, sent_q):
        both = jnp.concatenate([sent_p, sent_q]).reshape((2,) * bits_of("col") + (sub, -1))
        for bit in range(bits_of("col")):
            dim = bits_of("col") - 1 - bit
            both = jnp.where(my_bit("col", bit) == 0, both, jnp.flip(both, dim))
        return both.reshape(c.x.shape)[None]

    def far_pieces(got):
        names = [o for o in got if o >= 2]
        values = chain.enter(*[got[o] for o in names])
        values = list(values) if len(names) > 1 else [values]
        chain.leave(values[-1])
        for o, value in zip(names, values):
            got[o] = value
            got[o | 1] = swapped(value, "col", 0)

    near_names, far_names = [0, 1], list(range(2, n_col))
    d_p = out_first(d, [d_got[o] for o in near_names])
    u_inputs, u_pairs = make_pairs(u, inverse[1])
    d_p = out_second(*d_p)
    far_pieces(d_got)
    u_att = attend(u, u_inputs, inverse[1], u_pairs)
    u_got = gather(u_att, "col")
    u_got[1] = swapped(u_att, "col", 0)
    d_p = out_third(d, *d_p, near_names, 1)
    d_q = out_first(d, [d_got[o] for o in far_names])
    d_q = out_second(*d_q)
    u_p = out_first(u, [u_got[o] for o in near_names])
    far_pieces(u_got)
    u_p = out_second(*u_p)
    d_q = out_third(d, *d_q, far_names, 1)
    u_q = out_first(u, [u_got[o] for o in far_names])
    u_p = out_third(u, *u_p, near_names, -1)
    u_q = out_second(*u_q)
    u_q = out_third(u, *u_q, far_names, -1)
    return finish(d, d_p, d_q), finish(u, u_p, u_q)


def solution(mesh):
    tokens = P("section", "row", "col")
    into, out_of = P("section", "col", "row"), P("section", "row", "col")
    one = (tokens, P("section", "col"), into, into, into, out_of)
    return jax.shard_map(
        on_device, mesh=mesh, in_specs=one + one, out_specs=(tokens, tokens), check_vma=False
    )
```

profile of v0, /device:TPU:0, one launch (start us, length us, event | category | flops | bytes accessed | tf_op | source)
XLA Modules:
  0.0 330.0 jit_solution(13933144844035930660)
XLA Ops:
  1.2 2.6 collective-permute-start.2
  3.8 1.5 multiply_reduce_fusion.1
  5.3 1.5 multiply_reduce_fusion
  6.8 1.6 collective-permute-start.3
  9.7 4.7 %convolution_convert_fusion.3 = bf16[2,2,64,1280]{3,2,1,0:T(8,128)(2,1)} fusion(s32[]{:T(128)S(6)} %select_n.81, bf16[1,2,2,64,2048]{4,3,2,1,0:T(8,128)(2,1)S(1)} %bitcast.213, bf16[1,2,2,64,2048]{4,3,2,1,0:T(8,128)(2,1)S(1)} %bitcast.232, f32[2048]{0:T(1024)S(1)} %bitcast.271, bf16[2048,128]{1,0:T(8,128)(2,1)S(1)} %bitcast.256, ...), kind=kOutput, calls=%fused_computation.25 | convolution fusion | flops 1360330752 | bytes 8003588 | tf_op jit(solution)/shard_map/dot_general | solution.py:134
  14.5 1.6 fusion.32
  16.1 2.7 collective-permute-start.4
  18.7 1.9 collective-permute-done.4
  20.6 7.2 %collective-permute-done.2 = bf16[256,2048]{1,0:T(8,128)(2,1)} collective-permute-done((bf16[256,2048]{1,0:T(8,128)(2,1)}, bf16[256,2048]{1,0:T(8,128)(2,1)}, u32[]{:S(2)}, u32[]{:S(2)}) %collective-permute-start.2) | collective-permute-done | bytes 1048608 | tf_op jit(solution)/shard_map/ppermute | solution.py:19
  27.8 1.8 collective-permute-start.1
  29.9 1.5 collective-permute-start.10
  31.4 14.0 %collective-permute-done.1 = bf16[2,2,64,1280]{3,2,1,0:T(8,128)(2,1)} collective-permute-done((bf16[2,2,64,1280]{3,2,1,0:T(8,128)(2,1)}, bf16[2,2,64,1280]{3,2,1,0:T(8,128)(2,1)}, u32[]{:S(2)}, u32[]{:S(2)}) %collective-permute-start.1) | collective-permute-done | bytes 655392 | tf_op jit(solution)/shard_map/ppermute | solution.py:19
  45.4 1.9 add_convert_fusion.7
  47.3 4.5 %convolution_convert_fusion.2 = bf16[2,2,64,1280]{3,2,1,0:T(8,128)(2,1)S(1)} fusion(s32[]{:T(128)S(6)} %select_n.81, bf16[1,2,2,64,2048]{4,3,2,1,0:T(8,128)(2,1)} %bitcast.16, bf16[1,2,2,64,2048]{4,3,2,1,0:T(8,128)(2,1)} %bitcast.17, f32[2048]{0:T(1024)S(1)} %bitcast.273, bf16[2048,128]{1,0:T(8,128)(2,1)} %bitcast.255, bf16[2048,128]{1,0:T(8,128)(2,1)} %bitcast.259, ...), kind=kOutput, calls=%fused_computation.24 | convolution fusion | flops 1360330752 | bytes 8003588 | tf_op jit(solution)/shard_map/dot_general | solution.py:134
  51.9 1.8 collective-permute-start.6
  53.7 1.3 fusion.54
  55.0 1.6 fusion.33
  57.5 2.4 convolution_convert_fusion.1
  60.0 2.7 fusion.34
  62.7 5.7 %collective-permute-done.6 = bf16[2,2,64,1280]{3,2,1,0:T(8,128)(2,1)S(1)} collective-permute-done((bf16[2,2,64,1280]{3,2,1,0:T(8,128)(2,1)S(1)}, bf16[2,2,64,1280]{3,2,1,0:T(8,128)(2,1)S(1)}, u32[]{:S(2)}, u32[]{:S(2)}) %collective-permute-start.6) | collective-permute-done | bytes 655392 | tf_op jit(solution)/shard_map/ppermute | solution.py:19
  69.4 1.6 collective-permute-start.13
  71.1 1.9 collective-permute-done.13
  73.8 2.6 collective-permute-start.8
  76.7 1.6 collective-permute-start.18
  78.7 5.4 %convolution_convert_fusion = bf16[2,2,64,1280]{3,2,1,0:T(8,128)(2,1)} fusion(s32[]{:T(128)S(6)} %select_n.81, bf16[1,2,2,64,2048]{4,3,2,1,0:T(8,128)(2,1)} %bitcast.34, bf16[1,2,2,64,2048]{4,3,2,1,0:T(8,128)(2,1)} %bitcast.35, f32[2048]{0:T(1024)S(1)} %bitcast.277, bf16[2048,128]{1,0:T(8,128)(2,1)} %bitcast.263, bf16[2048,128]{1,0:T(8,128)(2,1)} %bitcast.267, ...), kind=kOutput, calls=%fused_computation.22 | convolution fusion | flops 1360330752 | bytes 8003588 | tf_op jit(solution)/shard_map/dot_general | solution.py:134
  84.1 1.5 fusion.44
  85.7 2.6 fusion.35
  88.3 11.3 %collective-permute-done.8 = bf16[2,1,64,1280]{3,2,1,0:T(8,128)(2,1)S(1)} collective-permute-done((bf16[2,1,64,1280]{3,2,1,0:T(8,128)(2,1)}, bf16[2,1,64,1280]{3,2,1,0:T(8,128)(2,1)S(1)}, u32[]{:S(2)}, u32[]{:S(2)}) %collective-permute-start.8) | collective-permute-done | bytes 327712 | tf_op jit(solution)/shard_map/ppermute | solution.py:19
  99.6 6.1 %collective-permute-done.9 = bf16[2,1,64,1280]{3,2,1,0:T(8,128)(2,1)S(1)} collective-permute-done((bf16[2,1,64,1280]{3,2,1,0:T(8,128)(2,1)S(1)}, bf16[2,1,64,1280]{3,2,1,0:T(8,128)(2,1)S(1)}, u32[]{:S(2)}, u32[]{:S(2)}) %collective-permute-start.9) | collective-permute-done | bytes 327712 | tf_op jit(solution)/shard_map/ppermute | solution.py:19
  106.0 1.9 convert_add_fusion.5
  107.9 1.4 collective-permute-start.20
  111.4 3.2 collective-permute-start.16
  114.6 1.5 collective-permute-start.17
  116.9 12.5 %collective-permute-done.15.rest_1_ = bf16[256,256]{1,0:T(8,128)(2,1)S(1)} collective-permute-done((bf16[256,256]{1,0:T(8,128)(2,1)S(1)}, bf16[256,256]{1,0:T(8,128)(2,1)S(1)}, u32[]{:S(2)}, u32[]{:S(2)}) %collective-permute-start.15) | collective-permute-done | bytes 131104 | tf_op jit(solution)/shard_map/ppermute | solution.py:23
  130.7 4.2 %collective-permute-done.17.rest_3_ = bf16[256,256]{1,0:T(8,128)(2,1)S(1)} collective-permute-done((bf16[256,256]{1,0:T(8,128)(2,1)S(1)}, bf16[256,256]{1,0:T(8,128)(2,1)S(1)}, u32[]{:S(2)}, u32[]{:S(2)}) %collective-permute-start.17) | collective-permute-done | bytes 131104 | tf_op jit(solution)/shard_map/ppermute | solution.py:23
  140.0 4.5 %shard_map.141 = bf16[256,1024]{1,0:T(8,128)(2,1)S(1)} custom-call(f32[128,1280]{1,0:T(8,128)S(1)} %bitcast.194, f32[128,1280]{1,0:T(8,128)S(1)} %bitcast.196, bf16[128,1280]{1,0:T(8,128)(2,1)S(1)} %bitcast.202, bf16[128,1280]{1,0:T(8,128)(2,1)S(1)} %bitcast.204, f32[256,1]{1,0:T(8,128)S(1)} %squeeze.144.inverse, f32[256,128]{1,0:T(8,128)S(1)} %pad_maximum_fusion.6.cosine, ...), custom_call_target="tpu_custom_call" | custom-call | flops 1073741824 | bytes 2097152 | tf_op jit(solution)/shard_map/pallas_call | solution.py:282
  144.6 2.3 convert_add_fusion.4
  146.9 9.3 %collective-permute-done.19 = bf16[256,1024]{1,0:T(8,128)(2,1)S(1)} collective-permute-done((bf16[256,1024]{1,0:T(8,128)(2,1)S(1)}, bf16[256,1024]{1,0:T(8,128)(2,1)S(1)}, u32[]{:S(2)}, u32[]{:S(2)}) %collective-permute-start.19) | collective-permute-done | bytes 524320 | tf_op jit(solution)/shard_map/ppermute | solution.py:19
  156.4 2.2 fusion.16
  158.6 2.1 constant_dynamic-slice_fusion
  161.0 2.9 collective-permute-start.28
  164.0 3.4 %fusion.12 = f32[2,128,2048]{2,1,0:T(8,128)S(1)} fusion(bf16[2,128,1024]{2,1,0:T(8,128)(2,1)S(1)} %bitcast.225, bf16[1,1024,2048]{2,1,0:T(8,128)(2,1)} %param.18), kind=kOutput, calls=%fused_computation.14 | convolution fusion | flops 1073741824 | bytes 6815744 | tf_op jit(solution)/shard_map/dot_general | solution.py:309
  167.4 29.8 %collective-permute-done.22 = bf16[2,1,64,1280]{3,2,1,0:T(8,128)(2,1)S(1)} collective-permute-done((bf16[2,1,64,1280]{3,2,1,0:T(8,128)(2,1)}, bf16[2,1,64,1280]{3,2,1,0:T(8,128)(2,1)S(1)}, u32[]{:S(2)}, u32[]{:S(2)}) %collective-permute-start.22) | collective-permute-done | bytes 327712 | tf_op jit(solution)/shard_map/ppermute | solution.py:19
  197.2 18.2 %collective-permute-done.23 = bf16[2,1,64,1280]{3,2,1,0:T(8,128)(2,1)S(1)} collective-permute-done((bf16[2,1,64,1280]{3,2,1,0:T(8,128)(2,1)}, bf16[2,1,64,1280]{3,2,1,0:T(8,128)(2,1)S(1)}, u32[]{:S(2)}, u32[]{:S(2)}) %collective-permute-start.23) | collective-permute-done | bytes 327712 | tf_op jit(solution)/shard_map/ppermute | solution.py:19
  215.7 1.8 collective-permute-start.26
  217.5 2.6 collective-permute-start.27
  220.1 1.6 add_bitcast_fusion.3
  221.8 1.5 collective-permute-start.24
  223.3 5.4 %collective-permute-done.26.rest_2_ = bf16[256,256]{1,0:T(8,128)(2,1)S(1)} collective-permute-done((bf16[256,256]{1,0:T(8,128)(2,1)S(1)}, bf16[256,256]{1,0:T(8,128)(2,1)S(1)}, u32[]{:S(2)}, u32[]{:S(2)}) %collective-permute-start.26) | collective-permute-done | bytes 131104 | tf_op jit(solution)/shard_map/ppermute | solution.py:23
  228.7 13.6 %shard_map.143 = bf16[256,1024]{1,0:T(8,128)(2,1)S(1)} custom-call(f32[128,1280]{1,0:T(8,128)S(1)} %bitcast.192, f32[128,1280]{1,0:T(8,128)S(1)} %bitcast.198, bf16[128,1280]{1,0:T(8,128)(2,1)S(1)} %bitcast.206, bf16[128,1280]{1,0:T(8,128)(2,1)S(1)} %bitcast.208, f32[256,1]{1,0:T(8,128)S(1)} %squeeze.145.inverse, f32[256,128]{1,0:T(8,128)S(1)} %pad_maximum_fusion.6.cosine, ...), custom_call_target="tpu_custom_call" | custom-call | flops 1073741824 | bytes 2097152 | tf_op jit(solution)/shard_map/pallas_call | solution.py:282
  246.2 2.5 collective-permute-start.33
  251.3 20.0 %collective-permute-done.33 = bf16[256,1024]{1,0:T(8,128)(2,1)S(1)} collective-permute-done((bf16[256,1024]{1,0:T(8,128)(2,1)S(1)}, bf16[256,1024]{1,0:T(8,128)(2,1)S(1)}, u32[]{:S(2)}, u32[]{:S(2)}) %collective-permute-start.33) | collective-permute-done | bytes 524320 | tf_op jit(solution)/shard_map/ppermute | solution.py:19
  271.5 2.3 fusion.22
  274.6 1.5 collective-permute-start.29
  276.1 1.5 collective-permute-start.32
  277.7 3.4 %fusion.4 = f32[2,128,2048]{2,1,0:T(8,128)S(1)} fusion(bf16[2,128,1024]{2,1,0:T(8,128)(2,1)S(1)} %bitcast.227, bf16[1,1024,2048]{2,1,0:T(8,128)(2,1)} %param.24), kind=kOutput, calls=%fused_computation.6 | convolution fusion | flops 1073741824 | bytes 6815744 | tf_op jit(solution)/shard_map/dot_general | solution.py:309
  281.2 1.3 slice_bitcast_fusion.2
  283.5 7.6 %collective-permute-done.32 = bf16[1,128,2048]{2,1,0:T(8,128)(2,1)S(1)} collective-permute-done((bf16[1,128,2048]{2,1,0:T(8,128)(2,1)}, bf16[1,128,2048]{2,1,0:T(8,128)(2,1)S(1)}, u32[]{:S(2)}, u32[]{:S(2)}) %collective-permute-start.32) | collective-permute-done | bytes 524320 | tf_op jit(solution)/shard_map/ppermute | solution.py:19
  292.1 3.1 collective-permute-done.38
  299.0 2.6 collective-permute-done.37
  302.9 1.5 collective-permute-start.41
  304.6 11.3 %collective-permute-done.41 = bf16[1,128,2048]{2,1,0:T(8,128)(2,1)S(1)} collective-permute-done((bf16[1,128,2048]{2,1,0:T(8,128)(2,1)S(1)}, bf16[1,128,2048]{2,1,0:T(8,128)(2,1)S(1)}, u32[]{:S(2)}, u32[]{:S(2)}) %collective-permute-start.41) | collective-permute-done | bytes 524320 | tf_op jit(solution)/shard_map/ppermute | solution.py:19
  316.1 1.6 collective-permute-start.42
  319.2 9.1 %collective-permute-done.42 = bf16[2,64,2048]{2,1,0:T(8,128)(2,1)S(1)} collective-permute-done((bf16[2,64,2048]{2,1,0:T(8,128)(2,1)S(1)}, bf16[2,64,2048]{2,1,0:T(8,128)(2,1)S(1)}, u32[]{:S(2)}, u32[]{:S(2)}) %collective-permute-start.42) | collective-permute-done | bytes 524320 | tf_op jit(solution)/shard_map/ppermute | solution.py:28
  (195 shorter events, 33.6 us)
Async XLA Ops:
  0.6 9.0 %copy-start.14 = (bf16[1,256,2048]{2,1,0:T(8,128)(2,1)S(1)}, bf16[1,256,2048]{2,1,0:T(8,128)(2,1)}, u32[]{:S(2)}) copy-start(bf16[1,256,2048]{2,1,0:T(8,128)(2,1)} %param.13) | copy-start | bytes 3145732
  0.6 9.0 %copy-start.37 = (f32[1,2048]{1,0:T(1,128)S(1)}, f32[1,2048]{1,0:T(1,128)}, u32[]{:S(2)}) copy-start(f32[1,2048]{1,0:T(1,128)} %param.14) | copy-start | bytes 24580
  0.7 9.0 %copy-start.27 = (bf16[1,2048,128]{2,1,0:T(8,128)(2,1)S(1)}, bf16[1,2048,128]{2,1,0:T(8,128)(2,1)}, u32[]{:S(2)}) copy-start(bf16[1,2048,128]{2,1,0:T(8,128)(2,1)} %param.17) | copy-start | bytes 1572868
  0.7 9.0 %copy-start.30 = (bf16[1,2048,128]{2,1,0:T(8,128)(2,1)S(1)}, bf16[1,2048,128]{2,1,0:T(8,128)(2,1)}, u32[]{:S(2)}) copy-start(bf16[1,2048,128]{2,1,0:T(8,128)(2,1)} %param.16) | copy-start | bytes 1572868
  0.7 7.8 %collective-permute-start = (bf16[256,2048]{1,0:T(8,128)(2,1)}, bf16[256,2048]{1,0:T(8,128)(2,1)S(1)}, u32[]{:S(2)}, u32[]{:S(2)}) collective-permute-start(bf16[256,2048]{1,0:T(8,128)(2,1)} %bitcast.209), channel_id=1, source_target_pairs={{0,4},{4,0},{8,12},{12,8},{1,5},{5,1},{9,13},{13,9},{2,6},{6,2},{1... | collective-permute-start | bytes 3145736 | tf_op jit(solution)/shard_map/ppermute | solution.py:19
  1.2 26.6 %collective-permute-start.2 = (bf16[256,2048]{1,0:T(8,128)(2,1)}, bf16[256,2048]{1,0:T(8,128)(2,1)}, u32[]{:S(2)}, u32[]{:S(2)}) collective-permute-start(bf16[256,2048]{1,0:T(8,128)(2,1)} %bitcast.210), channel_id=1, source_target_pairs={{0,8},{4,12},{8,0},{12,4},{1,9},{5,13},{9,1},{13,5},{2,10},{6,14},... | collective-permute-start | bytes 3145736 | tf_op jit(solution)/shard_map/ppermute | solution.py:19
  6.8 9.2 %collective-permute-start.3 = (f32[2,256]{1,0:T(2,128)S(1)}, f32[2,256]{1,0:T(2,128)S(1)}, u32[]{:S(2)}, u32[]{:S(2)}) collective-permute-start(f32[2,256]{1,0:T(2,128)S(1)} %pad_maximum_fusion.8), channel_id=1, source_target_pairs={{0,1},{1,0},{2,3},{3,2},{4,5},{5,4},{6,7},{7,6},{8,9},{9,8},{10,11... | collective-permute-start | bytes 6152 | tf_op jit(solution)/shard_map/ppermute | solution.py:19
  14.4 15.2 %copy-start.15 = (bf16[1,256,2048]{2,1,0:T(8,128)(2,1)S(1)}, bf16[1,256,2048]{2,1,0:T(8,128)(2,1)}, u32[]{:S(2)}) copy-start(bf16[1,256,2048]{2,1,0:T(8,128)(2,1)} %param.19) | copy-start | bytes 3145732
  16.1 4.5 %collective-permute-start.4 = (f32[2,256]{1,0:T(2,128)S(1)}, f32[2,256]{1,0:T(2,128)S(1)}, u32[]{:S(2)}, u32[]{:S(2)}) collective-permute-start(f32[2,256]{1,0:T(2,128)S(1)} %add.234), channel_id=1, source_target_pairs={{0,2},{1,3},{2,0},{3,1},{4,6},{5,7},{6,4},{7,5},{8,10},{9,11},{10,... | collective-permute-start | bytes 6152 | tf_op jit(solution)/shard_map/ppermute | solution.py:19
  27.8 19.5 %collective-permute-start.5 = (bf16[256,2048]{1,0:T(8,128)(2,1)}, bf16[256,2048]{1,0:T(8,128)(2,1)}, u32[]{:S(2)}, u32[]{:S(2)}) collective-permute-start(bf16[256,2048]{1,0:T(8,128)(2,1)} %collective-permute-done.2), channel_id=1, source_target_pairs={{0,4},{4,0},{8,12},{12,8},{1,5},{5,1},{9,13},{13,9},{2,6},{6,2},{1... | collective-permute-start | bytes 3145736 | tf_op jit(solution)/shard_map/ppermute | solution.py:19
  27.8 17.6 %collective-permute-start.1 = (bf16[2,2,64,1280]{3,2,1,0:T(8,128)(2,1)}, bf16[2,2,64,1280]{3,2,1,0:T(8,128)(2,1)}, u32[]{:S(2)}, u32[]{:S(2)}) collective-permute-start(bf16[2,2,64,1280]{3,2,1,0:T(8,128)(2,1)} %convolution_convert_fusion.3), channel_id=1, source_target_pairs={{0,1},{1,0},{2,3},{3,2},{4,5},{5,4},{6,7},{7,6},{8,9},{9,8},{10,11... | collective-permute-start | bytes 1966088 | tf_op jit(solution)/shard_map/ppermute | solution.py:19
  29.7 27.0 %collective-permute-start.7 = (bf16[256,2048]{1,0:T(8,128)(2,1)S(1)}, bf16[256,2048]{1,0:T(8,128)(2,1)S(1)}, u32[]{:S(2)}, u32[]{:S(2)}) collective-permute-start(bf16[256,2048]{1,0:T(8,128)(2,1)S(1)} %bitcast.214), channel_id=1, source_target_pairs={{0,4},{4,0},{8,12},{12,8},{1,5},{5,1},{9,13},{13,9},{2,6},{6,2},{1... | collective-permute-start | bytes 3145736 | tf_op jit(solution)/shard_map/ppermute | solution.py:19
  29.9 38.6 %collective-permute-start.10 = (bf16[256,2048]{1,0:T(8,128)(2,1)S(1)}, bf16[256,2048]{1,0:T(8,128)(2,1)}, u32[]{:S(2)}, u32[]{:S(2)}) collective-permute-start(bf16[256,2048]{1,0:T(8,128)(2,1)S(1)} %bitcast.215), channel_id=1, source_target_pairs={{0,8},{4,12},{8,0},{12,4},{1,9},{5,13},{9,1},{13,5},{2,10},{6,14},... | collective-permute-start | bytes 3145736 | tf_op jit(solution)/shard_map/ppermute | solution.py:19
  47.3 7.7 %copy-start.24 = (bf16[1,2048,1024]{2,1,0:T(8,128)(2,1)S(1)}, bf16[1,2048,1024]{2,1,0:T(8,128)(2,1)}, u32[]{:S(2)}) copy-start(bf16[1,2048,1024]{2,1,0:T(8,128)(2,1)} %param.15) | copy-start | bytes 12582916
  47.3 7.7 %copy-start.29 = (bf16[1,2048,128]{2,1,0:T(8,128)(2,1)S(1)}, bf16[1,2048,128]{2,1,0:T(8,128)(2,1)}, u32[]{:S(2)}) copy-start(bf16[1,2048,128]{2,1,0:T(8,128)(2,1)} %param.17) | copy-start | bytes 1572868
  47.3 7.7 %copy-start.32 = (bf16[1,2048,128]{2,1,0:T(8,128)(2,1)S(1)}, bf16[1,2048,128]{2,1,0:T(8,128)(2,1)}, u32[]{:S(2)}) copy-start(bf16[1,2048,128]{2,1,0:T(8,128)(2,1)} %param.16) | copy-start | bytes 1572868
  51.9 16.5 %collective-permute-start.6 = (bf16[2,2,64,1280]{3,2,1,0:T(8,128)(2,1)S(1)}, bf16[2,2,64,1280]{3,2,1,0:T(8,128)(2,1)S(1)}, u32[]{:S(2)}, u32[]{:S(2)}) collective-permute-start(bf16[2,2,64,1280]{3,2,1,0:T(8,128)(2,1)S(1)} %convolution_convert_fusion.2), channel_id=1, source_target_pairs={{0,1},{1,0},{2,3},{3,2},{4,5},{5,4},{6,7},{7,6},{8,9},{9,8},{10,11... | collective-permute-start | bytes 1966088 | tf_op jit(solution)/shard_map/ppermute | solution.py:19
  62.7 16.0 %copy-start.39 = (f32[1,2048]{1,0:T(1,128)S(1)}, f32[1,2048]{1,0:T(1,128)}, u32[]{:S(2)}) copy-start(f32[1,2048]{1,0:T(1,128)} %param.20) | copy-start | bytes 24580
  68.5 10.2 %collective-permute-start.11 = (bf16[256,2048]{1,0:T(8,128)(2,1)}, bf16[256,2048]{1,0:T(8,128)(2,1)}, u32[]{:S(2)}, u32[]{:S(2)}) collective-permute-start(bf16[256,2048]{1,0:T(8,128)(2,1)} %collective-permute-done.10), channel_id=1, source_target_pairs={{0,4},{4,0},{8,12},{12,8},{1,5},{5,1},{9,13},{13,9},{2,6},{6,2},{1... | collective-permute-start | bytes 3145736 | tf_op jit(solution)/shard_map/ppermute | solution.py:19
  69.4 3.7 %collective-permute-start.13 = (f32[2,256]{1,0:T(2,128)S(1)}, f32[2,256]{1,0:T(2,128)S(1)}, u32[]{:S(2)}, u32[]{:S(2)}) collective-permute-start(f32[2,256]{1,0:T(2,128)S(1)} %add.235), channel_id=1, source_target_pairs={{0,8},{4,12},{8,0},{12,4},{1,9},{5,13},{9,1},{13,5},{2,10},{6,14},... | collective-permute-start | bytes 6152 | tf_op jit(solution)/shard_map/ppermute | solution.py:19
  73.1 3.6 %collective-permute-start.14 = (f32[2,256]{1,0:T(2,128)S(1)}, f32[2,256]{1,0:T(2,128)S(1)}, u32[]{:S(2)}, u32[]{:S(2)}) collective-permute-start(f32[2,256]{1,0:T(2,128)S(1)} %collective-permute-done.13), channel_id=1, source_target_pairs={{0,4},{4,0},{8,12},{12,8},{1,5},{5,1},{9,13},{13,9},{2,6},{6,2},{1... | collective-permute-start | bytes 6152 | tf_op jit(solution)/shard_map/ppermute | solution.py:19
  73.1 5.3 %collective-permute-start.12 = (f32[2,256]{1,0:T(2,128)S(1)}, f32[2,256]{1,0:T(2,128)S(1)}, u32[]{:S(2)}, u32[]{:S(2)}) collective-permute-start(f32[2,256]{1,0:T(2,128)S(1)} %add.235), channel_id=1, source_target_pairs={{0,4},{4,0},{8,12},{12,8},{1,5},{5,1},{9,13},{13,9},{2,6},{6,2},{1... | collective-permute-start | bytes 6152 | tf_op jit(solution)/shard_map/ppermute | solution.py:19
  73.8 25.8 %collective-permute-start.8 = (bf16[2,1,64,1280]{3,2,1,0:T(8,128)(2,1)}, bf16[2,1,64,1280]{3,2,1,0:T(8,128)(2,1)S(1)}, u32[]{:S(2)}, u32[]{:S(2)}) collective-permute-start(bf16[2,1,64,1280]{3,2,1,0:T(8,128)(2,1)} %get-tuple-element.160), channel_id=1, source_target_pairs={{0,2},{1,3},{2,0},{3,1},{4,6},{5,7},{6,4},{7,5},{8,10},{9,11},{10,... | collective-permute-start | bytes 983048 | tf_op jit(solution)/shard_map/ppermute | solution.py:19
  76.4 29.3 %collective-permute-start.9 = (bf16[2,1,64,1280]{3,2,1,0:T(8,128)(2,1)S(1)}, bf16[2,1,64,1280]{3,2,1,0:T(8,128)(2,1)S(1)}, u32[]{:S(2)}, u32[]{:S(2)}) collective-permute-start(bf16[2,1,64,1280]{3,2,1,0:T(8,128)(2,1)S(1)} %get-tuple-element.158), channel_id=1, source_target_pairs={{0,2},{1,3},{2,0},{3,1},{4,6},{5,7},{6,4},{7,5},{8,10},{9,11},{10,... | collective-permute-start | bytes 983048 | tf_op jit(solution)/shard_map/ppermute | solution.py:19
  76.7 29.3 %collective-permute-start.18 = (bf16[2,2,64,1280]{3,2,1,0:T(8,128)(2,1)}, bf16[2,2,64,1280]{3,2,1,0:T(8,128)(2,1)}, u32[]{:S(2)}, u32[]{:S(2)}) collective-permute-start(bf16[2,2,64,1280]{3,2,1,0:T(8,128)(2,1)} %convolution_convert_fusion.1), channel_id=1, source_target_pairs={{0,1},{1,0},{2,3},{3,2},{4,5},{5,4},{6,7},{7,6},{8,9},{9,8},{10,11... | collective-permute-start | bytes 1966088 | tf_op jit(solution)/shard_map/ppermute | solution.py:19
  78.7 7.0 %copy-start.26 = (bf16[1,2048,1024]{2,1,0:T(8,128)(2,1)S(1)}, bf16[1,2048,1024]{2,1,0:T(8,128)(2,1)}, u32[]{:S(2)}) copy-start(bf16[1,2048,1024]{2,1,0:T(8,128)(2,1)} %param.21) | copy-start | bytes 12582916
  78.7 7.0 %copy-start.34 = (bf16[1,2048,128]{2,1,0:T(8,128)(2,1)S(1)}, bf16[1,2048,128]{2,1,0:T(8,128)(2,1)}, u32[]{:S(2)}) copy-start(bf16[1,2048,128]{2,1,0:T(8,128)(2,1)} %param.23) | copy-start | bytes 1572868
  78.7 7.0 %copy-start.36 = (bf16[1,2048,128]{2,1,0:T(8,128)(2,1)S(1)}, bf16[1,2048,128]{2,1,0:T(8,128)(2,1)}, u32[]{:S(2)}) copy-start(bf16[1,2048,128]{2,1,0:T(8,128)(2,1)} %param.22) | copy-start | bytes 1572868
  85.7 20.3 %copy-start.18 = (f32[2,2,64,1280]{3,2,1,0:T(8,128)S(1)}, f32[2,2,64,1280]{3,2,1,0:T(8,128)}, u32[]{:S(2)}) copy-start(f32[2,2,64,1280]{3,2,1,0:T(8,128)} %fusion.34) | copy-start | bytes 3932164
  105.9 24.2 %copy-start = (bf16[256,256]{1,0:T(8,128)(2,1)}, bf16[256,256]{1,0:T(8,128)(2,1)S(1)}, u32[]{:S(2)}) copy-start(bf16[256,256]{1,0:T(8,128)(2,1)S(1)} %shard_map.140.rest_0_) | copy-start | bytes 393220
  107.9 36.7 %collective-permute-start.20 = (bf16[2,2,64,1280]{3,2,1,0:T(8,128)(2,1)}, bf16[2,2,64,1280]{3,2,1,0:T(8,128)(2,1)}, u32[]{:S(2)}, u32[]{:S(2)}) collective-permute-start(bf16[2,2,64,1280]{3,2,1,0:T(8,128)(2,1)} %convolution_convert_fusion), channel_id=1, source_target_pairs={{0,1},{1,0},{2,3},{3,2},{4,5},{5,4},{6,7},{7,6},{8,9},{9,8},{10,11... | collective-permute-start | bytes 1966088 | tf_op jit(solution)/shard_map/ppermute | solution.py:19
  110.8 18.6 %collective-permute-start.15 = (bf16[256,256]{1,0:T(8,128)(2,1)S(1)}, bf16[256,256]{1,0:T(8,128)(2,1)S(1)}, u32[]{:S(2)}, u32[]{:S(2)}) collective-permute-start(bf16[256,256]{1,0:T(8,128)(2,1)S(1)} %shard_map.140.rest_0_), channel_id=1, source_target_pairs={{0,1},{1,0},{2,3},{3,2},{4,5},{5,4},{6,7},{7,6},{8,9},{9,8},{10,11... | collective-permute-start | bytes 393224 | tf_op jit(solution)/shard_map/ppermute | solution.py:23
  111.4 18.7 %collective-permute-start.16 = (bf16[256,256]{1,0:T(8,128)(2,1)S(1)}, bf16[256,256]{1,0:T(8,128)(2,1)S(1)}, u32[]{:S(2)}, u32[]{:S(2)}) collective-permute-start(bf16[256,256]{1,0:T(8,128)(2,1)S(1)} %shard_map.140.rest_0_), channel_id=1, source_target_pairs={{0,2},{1,3},{2,0},{3,1},{4,6},{5,7},{6,4},{7,5},{8,10},{9,11},{10,... | collective-permute-start | bytes 393224 | tf_op jit(solution)/shard_map/ppermute | solution.py:23
  114.6 20.3 %collective-permute-start.17 = (bf16[256,256]{1,0:T(8,128)(2,1)S(1)}, bf16[256,256]{1,0:T(8,128)(2,1)S(1)}, u32[]{:S(2)}, u32[]{:S(2)}) collective-permute-start(bf16[256,256]{1,0:T(8,128)(2,1)S(1)} %shard_map.140.rest_0_), channel_id=1, source_target_pairs={{0,3},{1,2},{2,1},{3,0},{4,7},{5,6},{6,5},{7,4},{8,11},{9,10},{10,... | collective-permute-start | bytes 393224 | tf_op jit(solution)/shard_map/ppermute | solution.py:23
  140.0 16.4 %copy-start.10 = (bf16[1,1024,2048]{2,1,0:T(8,128)(2,1)S(1)}, bf16[1,1024,2048]{2,1,0:T(8,128)(2,1)}, u32[]{:S(2)}) copy-start(bf16[1,1024,2048]{2,1,0:T(8,128)(2,1)} %param.18) | copy-start | bytes 12582916
  144.5 11.7 %collective-permute-start.19 = (bf16[256,1024]{1,0:T(8,128)(2,1)S(1)}, bf16[256,1024]{1,0:T(8,128)(2,1)S(1)}, u32[]{:S(2)}, u32[]{:S(2)}) collective-permute-start(bf16[256,1024]{1,0:T(8,128)(2,1)S(1)} %shard_map.141), channel_id=1, source_target_pairs={{0,1},{1,0},{2,3},{3,2},{4,5},{5,4},{6,7},{7,6},{8,9},{9,8},{10,11... | collective-permute-start | bytes 1572872 | tf_op jit(solution)/shard_map/ppermute | solution.py:19
  158.6 61.5 %collective-permute-start.21 = (bf16[2,128,2048]{2,1,0:T(8,128)(2,1)}, bf16[2,128,2048]{2,1,0:T(8,128)(2,1)}, u32[]{:S(2)}, u32[]{:S(2)}) collective-permute-start(bf16[2,128,2048]{2,1,0:T(8,128)(2,1)} %fusion.16), channel_id=1, source_target_pairs={{0,4},{4,0},{8,12},{12,8},{1,5},{5,1},{9,13},{13,9},{2,6},{6,2},{1... | collective-permute-start | bytes 3145736 | tf_op jit(solution)/shard_map/ppermute | solution.py:19
  160.9 36.3 %collective-permute-start.22 = (bf16[2,1,64,1280]{3,2,1,0:T(8,128)(2,1)}, bf16[2,1,64,1280]{3,2,1,0:T(8,128)(2,1)S(1)}, u32[]{:S(2)}, u32[]{:S(2)}) collective-permute-start(bf16[2,1,64,1280]{3,2,1,0:T(8,128)(2,1)} %get-tuple-element.157), channel_id=1, source_target_pairs={{0,2},{1,3},{2,0},{3,1},{4,6},{5,7},{6,4},{7,5},{8,10},{9,11},{10,... | collective-permute-start | bytes 983048 | tf_op jit(solution)/shard_map/ppermute | solution.py:19
  161.0 62.4 %collective-permute-start.28 = (bf16[256,1024]{1,0:T(8,128)(2,1)S(1)}, bf16[256,1024]{1,0:T(8,128)(2,1)S(1)}, u32[]{:S(2)}, u32[]{:S(2)}) collective-permute-start(bf16[256,1024]{1,0:T(8,128)(2,1)S(1)} %shard_map.141), channel_id=1, source_target_pairs={{0,2},{1,3},{2,0},{3,1},{4,6},{5,7},{6,4},{7,5},{8,10},{9,11},{10,... | collective-permute-start | bytes 1572872 | tf_op jit(solution)/shard_map/ppermute | solution.py:19
  163.9 51.6 %collective-permute-start.23 = (bf16[2,1,64,1280]{3,2,1,0:T(8,128)(2,1)}, bf16[2,1,64,1280]{3,2,1,0:T(8,128)(2,1)S(1)}, u32[]{:S(2)}, u32[]{:S(2)}) collective-permute-start(bf16[2,1,64,1280]{3,2,1,0:T(8,128)(2,1)} %get-tuple-element.155), channel_id=1, source_target_pairs={{0,2},{1,3},{2,0},{3,1},{4,6},{5,7},{6,4},{7,5},{8,10},{9,11},{10,... | collective-permute-start | bytes 983048 | tf_op jit(solution)/shard_map/ppermute | solution.py:19
  215.4 13.3 %copy-start.3 = (f32[256,1]{1,0:T(8,128)S(1)}, f32[256,1]{1,0:T(8,128)}, u32[]{:S(2)}) copy-start(f32[256,1]{1,0:T(8,128)} %convert_element_type.371.q_pos) | copy-start | bytes 3076
  215.6 7.7 %collective-permute-start.25 = (bf16[256,256]{1,0:T(8,128)(2,1)S(1)}, bf16[256,256]{1,0:T(8,128)(2,1)S(1)}, u32[]{:S(2)}, u32[]{:S(2)}) collective-permute-start(bf16[256,256]{1,0:T(8,128)(2,1)S(1)} %shard_map.142.rest_0_), channel_id=1, source_target_pairs={{0,1},{1,0},{2,3},{3,2},{4,5},{5,4},{6,7},{7,6},{8,9},{9,8},{10,11... | collective-permute-start | bytes 393224 | tf_op jit(solution)/shard_map/ppermute | solution.py:23
  215.7 13.0 %collective-permute-start.26 = (bf16[256,256]{1,0:T(8,128)(2,1)S(1)}, bf16[256,256]{1,0:T(8,128)(2,1)S(1)}, u32[]{:S(2)}, u32[]{:S(2)}) collective-permute-start(bf16[256,256]{1,0:T(8,128)(2,1)S(1)} %shard_map.142.rest_0_), channel_id=1, source_target_pairs={{0,2},{1,3},{2,0},{3,1},{4,6},{5,7},{6,4},{7,5},{8,10},{9,11},{10,... | collective-permute-start | bytes 393224 | tf_op jit(solution)/shard_map/ppermute | solution.py:23
  217.5 11.2 %collective-permute-start.27 = (bf16[256,256]{1,0:T(8,128)(2,1)S(1)}, bf16[256,256]{1,0:T(8,128)(2,1)S(1)}, u32[]{:S(2)}, u32[]{:S(2)}) collective-permute-start(bf16[256,256]{1,0:T(8,128)(2,1)S(1)} %shard_map.142.rest_0_), channel_id=1, source_target_pairs={{0,3},{1,2},{2,1},{3,0},{4,7},{5,6},{6,5},{7,4},{8,11},{9,10},{10,... | collective-permute-start | bytes 393224 | tf_op jit(solution)/shard_map/ppermute | solution.py:23
  221.8 20.8 %copy-start.20 = (bf16[1,64,2048]{2,1,0:T(8,128)(2,1)S(1)}, bf16[1,64,2048]{2,1,0:T(8,128)(2,1)}, u32[]{:S(2)}) copy-start(bf16[1,64,2048]{2,1,0:T(8,128)(2,1)} %get-tuple-element.171) | copy-start | bytes 786436
  221.8 20.7 %collective-permute-start.24 = (bf16[1,128,2048]{2,1,0:T(8,128)(2,1)S(1)}, bf16[1,128,2048]{2,1,0:T(8,128)(2,1)S(1)}, u32[]{:S(2)}, u32[]{:S(2)}) collective-permute-start(bf16[1,128,2048]{2,1,0:T(8,128)(2,1)S(1)} %fusion.76), channel_id=1, source_target_pairs={{0,8},{4,12},{8,0},{12,4},{1,9},{5,13},{9,1},{13,5},{2,10},{6,14},... | collective-permute-start | bytes 1572872 | tf_op jit(solution)/shard_map/ppermute | solution.py:19
  223.3 20.2 %collective-permute-start.30 = (bf16[256,1024]{1,0:T(8,128)(2,1)S(1)}, bf16[256,1024]{1,0:T(8,128)(2,1)S(1)}, u32[]{:S(2)}, u32[]{:S(2)}) collective-permute-start(bf16[256,1024]{1,0:T(8,128)(2,1)S(1)} %collective-permute-done.28), channel_id=1, source_target_pairs={{0,1},{1,0},{2,3},{3,2},{4,5},{5,4},{6,7},{7,6},{8,9},{9,8},{10,11... | collective-permute-start | bytes 1572872 | tf_op jit(solution)/shard_map/ppermute | solution.py:19
  246.1 4.0 %collective-permute-start.31 = (bf16[2,128,2048]{2,1,0:T(8,128)(2,1)S(1)}, bf16[2,128,2048]{2,1,0:T(8,128)(2,1)S(1)}, u32[]{:S(2)}, u32[]{:S(2)}) collective-permute-start(bf16[2,128,2048]{2,1,0:T(8,128)(2,1)S(1)} %fusion.19), channel_id=1, source_target_pairs={{0,4},{4,0},{8,12},{12,8},{1,5},{5,1},{9,13},{13,9},{2,6},{6,2},{1... | collective-permute-start | bytes 3145736 | tf_op jit(solution)/shard_map/ppermute | solution.py:19
  246.2 25.1 %collective-permute-start.33 = (bf16[256,1024]{1,0:T(8,128)(2,1)S(1)}, bf16[256,1024]{1,0:T(8,128)(2,1)S(1)}, u32[]{:S(2)}, u32[]{:S(2)}) collective-permute-start(bf16[256,1024]{1,0:T(8,128)(2,1)S(1)} %shard_map.143), channel_id=1, source_target_pairs={{0,1},{1,0},{2,3},{3,2},{4,5},{5,4},{6,7},{7,6},{8,9},{9,8},{10,11... | collective-permute-start | bytes 1572872 | tf_op jit(solution)/shard_map/ppermute | solution.py:19
  248.7 32.4 %collective-permute-start.35 = (bf16[256,1024]{1,0:T(8,128)(2,1)S(1)}, bf16[256,1024]{1,0:T(8,128)(2,1)}, u32[]{:S(2)}, u32[]{:S(2)}) collective-permute-start(bf16[256,1024]{1,0:T(8,128)(2,1)S(1)} %shard_map.143), channel_id=1, source_target_pairs={{0,2},{1,3},{2,0},{3,1},{4,6},{5,7},{6,4},{7,5},{8,10},{9,11},{10,... | collective-permute-start | bytes 1572872 | tf_op jit(solution)/shard_map/ppermute | solution.py:19
  250.1 21.4 %copy-start.12 = (bf16[1,1024,2048]{2,1,0:T(8,128)(2,1)S(1)}, bf16[1,1024,2048]{2,1,0:T(8,128)(2,1)}, u32[]{:S(2)}) copy-start(bf16[1,1024,2048]{2,1,0:T(8,128)(2,1)} %param.24) | copy-start | bytes 12582916
  250.5 23.3 %copy-start.17 = (f32[1,2,128,2048]{3,2,1,0:T(8,128)}, f32[1,2,128,2048]{3,2,1,0:T(8,128)S(1)}, u32[]{:S(2)}) copy-start(f32[1,2,128,2048]{3,2,1,0:T(8,128)S(1)} %add_bitcast_fusion.2) | copy-start | bytes 6291460
  273.7 8.8 %collective-permute-start.34 = (bf16[2,128,2048]{2,1,0:T(8,128)(2,1)}, bf16[2,128,2048]{2,1,0:T(8,128)(2,1)S(1)}, u32[]{:S(2)}, u32[]{:S(2)}) collective-permute-start(bf16[2,128,2048]{2,1,0:T(8,128)(2,1)} %fusion.22), channel_id=1, source_target_pairs={{0,4},{4,0},{8,12},{12,8},{1,5},{5,1},{9,13},{13,9},{2,6},{6,2},{1... | collective-permute-start | bytes 3145736 | tf_op jit(solution)/shard_map/ppermute | solution.py:19
  274.6 29.8 %collective-permute-start.29 = (bf16[2,64,2048]{2,1,0:T(8,128)(2,1)}, bf16[2,64,2048]{2,1,0:T(8,128)(2,1)S(1)}, u32[]{:S(2)}, u32[]{:S(2)}) collective-permute-start(bf16[2,64,2048]{2,1,0:T(8,128)(2,1)} %add_convert_fusion.3), channel_id=1, source_target_pairs={{0,16},{16,0},{1,17},{17,1},{2,18},{18,2},{3,19},{19,3},{4,20},{20... | collective-permute-start | bytes 1572872 | tf_op jit(solution)/shard_map/ppermute | solution.py:28
  276.1 15.0 %collective-permute-start.32 = (bf16[1,128,2048]{2,1,0:T(8,128)(2,1)}, bf16[1,128,2048]{2,1,0:T(8,128)(2,1)S(1)}, u32[]{:S(2)}, u32[]{:S(2)}) collective-permute-start(bf16[1,128,2048]{2,1,0:T(8,128)(2,1)} %fusion.77), channel_id=1, source_target_pairs={{0,8},{4,12},{8,0},{12,4},{1,9},{5,13},{9,1},{13,5},{2,10},{6,14},... | collective-permute-start | bytes 1572872 | tf_op jit(solution)/shard_map/ppermute | solution.py:19
  281.1 14.0 %collective-permute-start.38 = (bf16[256,1024]{1,0:T(8,128)(2,1)}, bf16[256,1024]{1,0:T(8,128)(2,1)S(1)}, u32[]{:S(2)}, u32[]{:S(2)}) collective-permute-start(bf16[256,1024]{1,0:T(8,128)(2,1)} %collective-permute-done.35), channel_id=1, source_target_pairs={{0,1},{1,0},{2,3},{3,2},{4,5},{5,4},{6,7},{7,6},{8,9},{9,8},{10,11... | collective-permute-start | bytes 1572872 | tf_op jit(solution)/shard_map/ppermute | solution.py:19
  282.5 8.8 %copy-start.19 = (bf16[1,64,2048]{2,1,0:T(8,128)(2,1)S(1)}, bf16[1,64,2048]{2,1,0:T(8,128)(2,1)}, u32[]{:S(2)}) copy-start(bf16[1,64,2048]{2,1,0:T(8,128)(2,1)} %get-tuple-element.169) | copy-start | bytes 786436
  282.9 18.7 %collective-permute-start.37 = (bf16[1,128,2048]{2,1,0:T(8,128)(2,1)S(1)}, bf16[1,128,2048]{2,1,0:T(8,128)(2,1)S(1)}, u32[]{:S(2)}, u32[]{:S(2)}) collective-permute-start(bf16[1,128,2048]{2,1,0:T(8,128)(2,1)S(1)} %fusion.78), channel_id=1, source_target_pairs={{0,8},{4,12},{8,0},{12,4},{1,9},{5,13},{9,1},{13,5},{2,10},{6,14},... | collective-permute-start | bytes 1572872 | tf_op jit(solution)/shard_map/ppermute | solution.py:19
  291.2 5.1 %copy-start.13 = (bf16[1,1024,2048]{2,1,0:T(8,128)(2,1)S(1)}, bf16[1,1024,2048]{2,1,0:T(8,128)(2,1)}, u32[]{:S(2)}) copy-start(bf16[1,1024,2048]{2,1,0:T(8,128)(2,1)} %param.24) | copy-start | bytes 12582916
  291.4 13.0 %collective-permute-start.36 = (bf16[2,64,2048]{2,1,0:T(8,128)(2,1)S(1)}, bf16[2,64,2048]{2,1,0:T(8,128)(2,1)S(1)}, u32[]{:S(2)}, u32[]{:S(2)}) collective-permute-start(bf16[2,64,2048]{2,1,0:T(8,128)(2,1)S(1)} %add_convert_fusion.2), channel_id=1, source_target_pairs={{0,16},{16,0},{1,17},{17,1},{2,18},{18,2},{3,19},{19,3},{4,20},{20... | collective-permute-start | bytes 1572872 | tf_op jit(solution)/shard_map/ppermute | solution.py:28
  297.6 4.9 %collective-permute-start.40 = (bf16[2,128,2048]{2,1,0:T(8,128)(2,1)S(1)}, bf16[2,128,2048]{2,1,0:T(8,128)(2,1)S(1)}, u32[]{:S(2)}, u32[]{:S(2)}) collective-permute-start(bf16[2,128,2048]{2,1,0:T(8,128)(2,1)S(1)} %fusion.25), channel_id=1, source_target_pairs={{0,4},{4,0},{8,12},{12,8},{1,5},{5,1},{9,13},{13,9},{2,6},{6,2},{1... | collective-permute-start | bytes 3145736 | tf_op jit(solution)/shard_map/ppermute | solution.py:19
  302.0 17.2 %collective-permute-start.39 = (bf16[2,64,2048]{2,1,0:T(8,128)(2,1)S(1)}, bf16[2,64,2048]{2,1,0:T(8,128)(2,1)S(1)}, u32[]{:S(2)}, u32[]{:S(2)}) collective-permute-start(bf16[2,64,2048]{2,1,0:T(8,128)(2,1)S(1)} %add_convert_fusion.1), channel_id=1, source_target_pairs={{0,16},{16,0},{1,17},{17,1},{2,18},{18,2},{3,19},{19,3},{4,20},{20... | collective-permute-start | bytes 1572872 | tf_op jit(solution)/shard_map/ppermute | solution.py:28
  302.9 13.0 %collective-permute-start.41 = (bf16[1,128,2048]{2,1,0:T(8,128)(2,1)S(1)}, bf16[1,128,2048]{2,1,0:T(8,128)(2,1)S(1)}, u32[]{:S(2)}, u32[]{:S(2)}) collective-permute-start(bf16[1,128,2048]{2,1,0:T(8,128)(2,1)S(1)} %fusion.79), channel_id=1, source_target_pairs={{0,8},{4,12},{8,0},{12,4},{1,9},{5,13},{9,1},{13,5},{2,10},{6,14},... | collective-permute-start | bytes 1572872 | tf_op jit(solution)/shard_map/ppermute | solution.py:19
  316.1 12.1 %collective-permute-start.42 = (bf16[2,64,2048]{2,1,0:T(8,128)(2,1)S(1)}, bf16[2,64,2048]{2,1,0:T(8,128)(2,1)S(1)}, u32[]{:S(2)}, u32[]{:S(2)}) collective-permute-start(bf16[2,64,2048]{2,1,0:T(8,128)(2,1)S(1)} %add_convert_fusion), channel_id=1, source_target_pairs={{0,16},{16,0},{1,17},{17,1},{2,18},{18,2},{3,19},{19,3},{4,20},{20... | collective-permute-start | bytes 1572872 | tf_op jit(solution)/shard_map/ppermute | solution.py:28
  (19 other events, 42.9 us)
where the time goes:
time: 336 us; the launch traced here: 330 us
  waiting for transfers between devices  181 us (54%)
  starting transfers between devices  46 us (14%)
  matrix products  42 us (12%)
  other arithmetic  24.4 us (7%)
  Pallas kernels  18.5 us (6%)
  local copies, waits for them, and re-layouts  16 us (5%)
    ppermute x33, waiting for transfers between devices, swapped(): lax.ppermute(value, axis, [(i, i ^ 1 << bit) for i in range(lax.axis_size...  150 us
    ppermute x33, starting transfers between devices, swapped(): lax.ppermute(value, axis, [(i, i ^ 1 << bit) for i in range(lax.axis_size...  32 us
    dot_general x8, matrix products, project(): out = jnp.dot(rows, self.w, preferred_element_type=F32)  25.5 us
    ppermute x6, waiting for transfers between devices, crossed(): lax.ppermute(value, axis, [(i, i ^ bits) for i in range(lax.axis_size(axi...  22.1 us
    pallas_call x2, Pallas kernels, attend(): whole(functools.partial(attention_kernel, qw, kvw, n_col), jax.ShapeDtype...  18.1 us
    dot_general x8, matrix products, dot(): out = jnp.dot(value.reshape(-1, qw), c.wo, preferred_element_type=F32)  16.4 us
    ppermute x6, starting transfers between devices, crossed(): lax.ppermute(value, axis, [(i, i ^ bits) for i in range(lax.axis_size(axi...  9.71 us
    ppermute x4, waiting for transfers between devices, from_behind(): lax.ppermute(value, axis, [(i, (i + steps) % count) for i in range(count)])  9.06 us
  transfers between devices with their start and end apart: 43, of which 20 were waited for; matrix products, arithmetic and copies ran while one was open for 20% of the time, Pallas kernels for 6%

commit v1 on v0

--- a/solution.py
+++ b/solution.py
@@ -100,7 +100,7 @@
         out[:, columns] = (mixed / total).astype(BF16)
 
 
-def gather(block, axis, after_far=None):
+def gather(block, axis):
     blocks = {0: block}
     for bit in range(1, bits_of(axis)):
         for o in list(blocks):
@@ -121,7 +121,6 @@
         self.n_row, self.n_col = lax.axis_size("row"), lax.axis_size("col")
         self.sub = x.shape[0] // self.n_col
         self.keep, self.arrived = [], []
-        self.first, self.second = [None, None], [None, None]
 
     def halves(self, block_list):
         low = my_bit("col", 0)
@@ -189,7 +188,7 @@
     d_blocks = gather(d.x, "row")
     d_blocks[1] = swapped(d.x, "row", 0)
     squares = jnp.stack([jnp.sum(jnp.square(c.x.astype(F32)), axis=1) for c in (d, u)])
-    other = swapped(squares, "col", 0)
+    squares = lax.all_gather(squares, ("row", "col")).reshape(n_row, n_col, 2, block)
 
     def send_first(c, group, blocks_):
         send, kept = c.halves(chain.enter(*blocks_))
@@ -198,31 +197,6 @@
 
     def keep_first(c, kept, token):
         return c.project(tie(kept, token))
-
-    product, kept = send_first(d, 0, [d_blocks[0], d_blocks[1]])
-    d_arr_a = swapped(product, "col", 0)
-    d_tot_a = keep_first(d, kept, product)
-    chain.leave(d_tot_a)
-    squares, other = chain.enter(squares, other)
-    squares = squares + other
-    for bit in range(1, bits_of("col")):
-        squares = squares + swapped(squares, "col", bit)
-    chain.leave(squares)
-    u_near = swapped(chain.enter(u.x), "row", 0)
-
-    far = [o for o in d_blocks if o >= 2]
-    d_far = chain.enter(*[d_blocks[o] for o in far])
-    d_far = list(d_far) if len(far) > 1 else [d_far]
-    u_blocks = gather(tie(u.x, *d_far), "row")
-    u_blocks[1] = u_near
-    for o, value in zip(far, d_far):
-        d_blocks[o] = value
-        d_blocks[o | 1] = swapped(value, "row", 0)
-    chain.leave(d_far[-1])
-    sq = {0: squares}
-    for bit in range(1, bits_of("row")):
-        for o in list(sq):
-            sq[o | 1 << bit] = swapped(tie(sq[o], *d_far), "row", bit)
 
     def second(c, total, arrived):
         total, arrived = chain.enter(total, arrived)
@@ -235,36 +209,50 @@
         c.keep.append(kept)
         c.arrived.append(arrived)
 
+    def settle(c):
+        c.arrived[-1] = chain.enter(c.arrived[-1])
+        chain.leave(c.arrived[-1])
+
+    def take_far(blocks_):
+        values = chain.enter(*[blocks_[o] for o in far])
+        values = list(values) if len(far) > 1 else [values]
+        for o, value in zip(far, values):
+            blocks_[o] = value
+            blocks_[o | 1] = swapped(value, "row", 0)
+        chain.leave(values[-1])
+        return values
+
+    far = [o for o in d_blocks if o >= 2]
+    far_order = [o for o in order if o >= 2]
+
+    product, kept = send_first(d, 0, [d_blocks[0], d_blocks[1]])
+    d_arr_a = swapped(product, "col", 0)
+    d_tot_a = keep_first(d, kept, product)
+    u_near = swapped(tie(u.x, product), "row", 0)
+    chain.leave(d_tot_a)
+    u_prod_a, kept = send_first(u, 0, [u.x, u_near])
+    u_tot_a = keep_first(u, kept, u_prod_a)
+    chain.leave(u_tot_a)
     second(d, d_tot_a, d_arr_a)
 
-    far_order = [o for o in order if o >= 2]
+    d_far = take_far(d_blocks)
+    u_blocks = gather(tie(u.x, *d_far), "row")
     product, kept = send_first(d, 1, [d_blocks[o] for o in far_order])
     d_arr_b = swapped(product, "col", 0)
     d_tot_b = keep_first(d, kept, product)
     chain.leave(d_tot_b)
-
-    u_prod_a, kept = send_first(u, 0, [u_blocks[0], u_blocks[1]])
-    u_tot_a = keep_first(u, kept, u_prod_a)
-    chain.leave(u_tot_a)
-
+    settle(d)
     second(d, d_tot_b, d_arr_b)
     u_arr_a = swapped(tie(u_prod_a, chain.token), "col", 0)
 
-    u_far = chain.enter(*[u_blocks[o] for o in far])
-    u_far = list(u_far) if len(far) > 1 else [u_far]
-    for o, value in zip(far, u_far):
-        u_blocks[o] = value
-        u_blocks[o | 1] = swapped(value, "row", 0)
-    chain.leave(u_far[-1])
-    for o in list(sq):
-        sq[o | 1] = swapped(tie(sq[o], *u_far), "row", 0)
+    take_far(u_blocks)
     u_prod_b, kept = send_first(u, 1, [u_blocks[o] for o in far_order])
     u_tot_b = keep_first(u, kept, u_prod_b)
     chain.leave(u_tot_b)
 
-    sums = jnp.stack([sq[o] for o in order])
-    sums = pick(sums.reshape(n_row, 2, n_col, sub), z, 2)
-    inverse = lax.rsqrt(sums / features + EPSILON).transpose(1, 0, 2).reshape(2, rows, 1)
+    sums = jnp.sum(pick(squares.reshape(n_row, n_col, 2, n_col, sub), z, 3), axis=1)
+    inverse = lax.rsqrt(sums / features + EPSILON)
+    inverse = jnp.stack([pick(inverse, r ^ o, 0) for o in order], axis=1).reshape(2, rows, 1)
 
     def make_pairs(c, scale):
         inputs = chain.enter(*c.kernel_rows())
@@ -290,15 +278,14 @@
         chain.leave(out)
         return out
 
-    d_inputs, d_pairs = make_pairs(d, inverse[0])
     second(u, u_tot_a, u_arr_a)
     u_arr_b = swapped(tie(u_prod_b, chain.token), "col", 0)
+    d_inputs, d_pairs = make_pairs(d, inverse[0])
+    settle(u)
     d_att = attend(d, d_inputs, inverse[0], d_pairs)
     d_got = gather(d_att, "col")
     d_got[1] = swapped(d_att, "col", 0)
     second(u, u_tot_b, u_arr_b)
-
-    order_rows = jnp.array(order)
 
     def out_first(c, pieces):
         pieces = chain.enter(*pieces)
@@ -350,18 +337,18 @@
             got[o | 1] = swapped(value, "col", 0)
 
     near_names, far_names = [0, 1], list(range(2, n_col))
+    far_pieces(d_got)
     d_p = out_first(d, [d_got[o] for o in near_names])
     u_inputs, u_pairs = make_pairs(u, inverse[1])
     d_p = out_second(*d_p)
-    far_pieces(d_got)
     u_att = attend(u, u_inputs, inverse[1], u_pairs)
     u_got = gather(u_att, "col")
     u_got[1] = swapped(u_att, "col", 0)
+    d_q = out_first(d, [d_got[o] for o in far_names])
     d_p = out_third(d, *d_p, near_names, 1)
-    d_q = out_first(d, [d_got[o] for o in far_names])
     d_q = out_second(*d_q)
+    far_pieces(u_got)
     u_p = out_first(u, [u_got[o] for o in near_names])
-    far_pieces(u_got)
     u_p = out_second(*u_p)
     d_q = out_third(d, *d_q, far_names, 1)
     u_q = out_first(u, [u_got[o] for o in far_names])

time: 336 us -> 320 us (0.952)
  blocking collectives: 0 us -> 33.7 us
  waiting for transfers between devices: 181 us -> 165 us
  starting transfers between devices: 46 us -> 34.6 us
  local copies, waits for them, and re-layouts: 16 us -> 6.26 us
  Pallas kernels: 18.5 us -> 10.6 us
  other arithmetic: 24.4 us -> 20.4 us
    all_gather x0 -> x1, blocking collectives: none -> 33.7 us  [on_device(): lax.all_gather(squares, ('row', 'col')).reshape(n_row, n_col, 2, block)]
    ppermute x33 -> x28, waiting for transfers between devices: 150 us -> 133 us  [swapped(): lax.ppermute(value, axis, [(i, i ^ 1 << bit) for i in range(lax.axis_size...]
    ppermute x33 -> x28, starting transfers between devices: 32 us -> 21.4 us  [swapped(): lax.ppermute(value, axis, [(i, i ^ 1 << bit) for i in range(lax.axis_size...]
    pallas_call x2, Pallas kernels: 18.1 us -> 10.2 us  [attend(): whole(functools.partial(attention_kernel, qw, kvw, n_col), jax.ShapeDtype...]
    unnamed x80 -> x44, local copies, waits for them, and re-layouts: 8.61 us -> 1.42 us
    dot_general x8, matrix products: 25.5 us -> 29 us  [project(): out = jnp.dot(rows, self.w, preferred_element_type=F32)]
  transfers between devices with their start and end apart: 43 -> 38, of which waited for: 20 -> 21; matrix products, arithmetic and copies ran while one was open for 20% -> 18% of each run, Pallas kernels for 6% -> 3%
where the time goes in v1:
time: 320 us; the launch traced here: 315 us
  waiting for transfers between devices  165 us (52%)
  matrix products  42.2 us (13%)
  starting transfers between devices  34.6 us (11%)
  blocking collectives  33.7 us (11%)
  other arithmetic  20.4 us (6%)
  Pallas kernels  10.6 us (3%)
  local copies, waits for them, and re-layouts  6.26 us (2%)
    ppermute x28, waiting for transfers between devices, swapped(): lax.ppermute(value, axis, [(i, i ^ 1 << bit) for i in range(lax.axis_size...  133 us
    all_gather x1, blocking collectives, on_device(): lax.all_gather(squares, ('row', 'col')).reshape(n_row, n_col, 2, block)  33.7 us
    dot_general x8, matrix products, project(): out = jnp.dot(rows, self.w, preferred_element_type=F32)  29 us
    ppermute x6, waiting for transfers between devices, crossed(): lax.ppermute(value, axis, [(i, i ^ bits) for i in range(lax.axis_size(axi...  22.3 us
    ppermute x28, starting transfers between devices, swapped(): lax.ppermute(value, axis, [(i, i ^ 1 << bit) for i in range(lax.axis_size...  21.4 us
    dot_general x8, matrix products, dot(): out = jnp.dot(value.reshape(-1, qw), c.wo, preferred_element_type=F32)  13.3 us
    pallas_call x2, Pallas kernels, attend(): whole(functools.partial(attention_kernel, qw, kvw, n_col), jax.ShapeDtype...  10.2 us
    ppermute x4, waiting for transfers between devices, from_behind(): lax.ppermute(value, axis, [(i, (i + steps) % count) for i in range(count)])  9.65 us
  transfers between devices with their start and end apart: 38, of which 21 were waited for; matrix products, arithmetic and copies ran while one was open for 18% of the time, Pallas kernels for 3%

profile of v1, /device:TPU:0, one launch (start us, length us, event | category | flops | bytes accessed | tf_op | source)
XLA Modules:
  0.0 314.8 jit_solution(11228079320462270830)
XLA Ops:
  1.1 2.5 collective-permute-done
  3.7 4.6 %convolution_convert_fusion.3 = bf16[2,2,64,1280]{3,2,1,0:T(8,128)(2,1)S(1)} fusion(s32[]{:T(128)S(6)} %select_n.94, bf16[1,2,2,64,2048]{4,3,2,1,0:T(8,128)(2,1)} %bitcast.217, bf16[1,2,2,64,2048]{4,3,2,1,0:T(8,128)(2,1)S(1)} %bitcast.237, f32[2048]{0:T(1024)} %bitcast.275, bf16[2048,128]{1,0:T(8,128)(2,1)} %bitcast.259, bf16[2048,128]{1,0:T(8,128)(2,1)} %bitcast.263, ...), kind=kOutput, calls=%fused_computation.25 | convolution fusion | flops 1360330752 | bytes 8003588 | tf_op jit(solution)/shard_map/dot_general | solution.py:133
  8.7 2.6 collective-permute-start.3
  11.4 1.6 collective-permute-start.1
  12.9 1.1 fusion.59
  14.1 4.2 %fusion.32 = f32[2,2,64,1280]{3,2,1,0:T(8,128)S(1)} fusion(bf16[2,2,64,2048]{3,2,1,0:T(8,128)(2,1)S(1)} %fusion.59, f32[2048]{0:T(1024)S(1)} %bitcast.276, bf16[2048,128]{1,0:T(8,128)(2,1)} %bitcast.260, bf16[2048,128]{1,0:T(8,128)(2,1)} %bitcast.264, bf16[2048,1024]{1,0:T(8,128)(2,1)} %bitcast.252), kind=kOutput, calls=%fused_computation.64 | convolution fusion | flops 1359478784 | bytes 7610368 | tf_op jit(solution)/shard_map/dot_general | solution.py:133
  18.4 3.7 %convolution_convert_fusion.2 = bf16[2,2,64,1280]{3,2,1,0:T(8,128)(2,1)} fusion(s32[]{:T(128)S(6)} %select_n.94, bf16[1,2,2,64,2048]{4,3,2,1,0:T(8,128)(2,1)} %bitcast.13, bf16[1,2,2,64,2048]{4,3,2,1,0:T(8,128)(2,1)} %bitcast.14, f32[2048]{0:T(1024)S(1)} %bitcast.279, bf16[2048,128]{1,0:T(8,128)(2,1)S(1)} %bitcast.268, bf16[2048,128]{1,0:T(8,128)(2,1)S(1)} %bitcast.272, ...), kind=kOutput, calls=%fused_computation.24 | convolution fusion | flops 1360330752 | bytes 8003588 | tf_op jit(solution)/shard_map/dot_general | solution.py:133
  22.1 1.3 fusion.54
  23.4 2.7 fusion.33
  26.0 2.0 collective-permute-done.1
  28.9 6.1 %collective-permute-done.3 = bf16[256,2048]{1,0:T(8,128)(2,1)S(1)} collective-permute-done((bf16[256,2048]{1,0:T(8,128)(2,1)S(1)}, bf16[256,2048]{1,0:T(8,128)(2,1)S(1)}, u32[]{:S(2)}, u32[]{:S(2)}) %collective-permute-start.3) | collective-permute-done | bytes 1048608 | tf_op jit(solution)/shard_map/ppermute | solution.py:19
  35.0 1.5 multiply_reduce_fusion
  36.9 33.7 %all-gather.1 = f32[16,2,256]{2,1,0:T(2,128)S(1)} all-gather(f32[1,2,256]{2,1,0:T(2,128)S(1)} %maximum_bitcast_fusion.2), channel_id=2, replica_groups=mesh['section'=2,'row'=4,'col'=4] {'row','col'}, dimensions={0}, use_global_device_ids=true | all-gather | bytes 34816 | tf_op jit(solution)/shard_map/all_gather | solution.py:191
  71.5 4.4 %convolution_convert_fusion.1 = bf16[2,2,64,1280]{3,2,1,0:T(8,128)(2,1)S(1)} fusion(s32[]{:T(128)S(6)} %select_n.94, bf16[1,2,2,64,2048]{4,3,2,1,0:T(8,128)(2,1)S(1)} %bitcast.233, bf16[1,2,2,64,2048]{4,3,2,1,0:T(8,128)(2,1)} %bitcast.25, f32[2048]{0:T(1024)S(1)} %bitcast.277, bf16[2048,128]{1,0:T(8,128)(2,1)} %bitcast.261, ...), kind=kOutput, calls=%fused_computation.23 | convolution fusion | flops 1360330752 | bytes 8003588 | tf_op jit(solution)/shard_map/dot_general | solution.py:133
  76.0 1.1 fusion.49
  77.1 1.6 fusion.34
  78.7 6.3 %collective-permute-done.6 = bf16[2,1,64,1280]{3,2,1,0:T(8,128)(2,1)S(1)} collective-permute-done((bf16[2,1,64,1280]{3,2,1,0:T(8,128)(2,1)}, bf16[2,1,64,1280]{3,2,1,0:T(8,128)(2,1)S(1)}, u32[]{:S(2)}, u32[]{:S(2)}) %collective-permute-start.6) | collective-permute-done | bytes 327712 | tf_op jit(solution)/shard_map/ppermute | solution.py:19
  85.0 12.5 %collective-permute-done.5 = bf16[2,2,64,1280]{3,2,1,0:T(8,128)(2,1)S(1)} collective-permute-done((bf16[2,2,64,1280]{3,2,1,0:T(8,128)(2,1)S(1)}, bf16[2,2,64,1280]{3,2,1,0:T(8,128)(2,1)S(1)}, u32[]{:S(2)}, u32[]{:S(2)}) %collective-permute-start.5) | collective-permute-done | bytes 655392 | tf_op jit(solution)/shard_map/ppermute | solution.py:19
  100.2 2.0 collective-permute-start.8
  102.3 5.2 %convolution_convert_fusion = bf16[2,2,64,1280]{3,2,1,0:T(8,128)(2,1)} fusion(s32[]{:T(128)S(6)} %select_n.94, bf16[1,2,2,64,2048]{4,3,2,1,0:T(8,128)(2,1)S(1)} %bitcast.235, bf16[1,2,2,64,2048]{4,3,2,1,0:T(8,128)(2,1)} %bitcast.33, f32[2048]{0:T(1024)S(1)} %bitcast.281, bf16[2048,128]{1,0:T(8,128)(2,1)} %bitcast.267, bf16[2048,128]{1,0:T(8,128)(2,1)} %bitcast.271, ...), kind=kOutput, calls=%fused_computation.22 | convolution fusion | flops 1360330752 | bytes 8003588 | tf_op jit(solution)/shard_map/dot_general | solution.py:133
  107.5 1.1 fusion.44
  108.7 2.7 fusion.35
  111.3 13.3 %collective-permute-done.8 = bf16[2,2,64,1280]{3,2,1,0:T(8,128)(2,1)S(1)} collective-permute-done((bf16[2,2,64,1280]{3,2,1,0:T(8,128)(2,1)}, bf16[2,2,64,1280]{3,2,1,0:T(8,128)(2,1)S(1)}, u32[]{:S(2)}, u32[]{:S(2)}) %collective-permute-start.8) | collective-permute-done | bytes 655392 | tf_op jit(solution)/shard_map/ppermute | solution.py:19
  126.0 2.4 collective-permute-start.17
  128.8 2.1 collective-permute-start.12
  130.8 2.3 collective-permute-start.13
  133.3 9.8 %collective-permute-done.14 = bf16[2,1,64,1280]{3,2,1,0:T(8,128)(2,1)S(1)} collective-permute-done((bf16[2,1,64,1280]{3,2,1,0:T(8,128)(2,1)}, bf16[2,1,64,1280]{3,2,1,0:T(8,128)(2,1)S(1)}, u32[]{:S(2)}, u32[]{:S(2)}) %collective-permute-start.14) | collective-permute-done | bytes 327712 | tf_op jit(solution)/shard_map/ppermute | solution.py:19
  143.1 13.7 %collective-permute-done.11.rest_1_ = bf16[256,256]{1,0:T(8,128)(2,1)} collective-permute-done((bf16[256,256]{1,0:T(8,128)(2,1)S(1)}, bf16[256,256]{1,0:T(8,128)(2,1)}, u32[]{:S(2)}, u32[]{:S(2)}) %collective-permute-start.11) | collective-permute-done | bytes 131104 | tf_op jit(solution)/shard_map/ppermute | solution.py:23
  156.7 1.8 collective-permute-done.13.rest_3_
  158.5 0.9 copy-done
  159.4 5.7 %shard_map.141 = bf16[256,1024]{1,0:T(8,128)(2,1)S(1)} custom-call(f32[128,1280]{1,0:T(8,128)S(1)} %bitcast.199, f32[128,1280]{1,0:T(8,128)S(1)} %bitcast.203, bf16[128,1280]{1,0:T(8,128)(2,1)S(1)} %bitcast.211, bf16[128,1280]{1,0:T(8,128)(2,1)S(1)} %bitcast.213, f32[256,1]{1,0:T(8,128)S(1)} %squeeze.149.inverse, f32[256,128]{1,0:T(8,128)S(1)} %pad_maximum_fusion.6.cosine, ...), custom_call_target="tpu_custom_call" | custom-call | flops 1073741824 | bytes 2097152 | tf_op jit(solution)/shard_map/pallas_call | solution.py:270
  165.2 2.2 collective-permute-start.15
  167.4 2.5 convert_add_fusion.4
  169.9 19.0 %collective-permute-done.16 = bf16[256,1024]{1,0:T(8,128)(2,1)S(1)} collective-permute-done((bf16[256,1024]{1,0:T(8,128)(2,1)S(1)}, bf16[256,1024]{1,0:T(8,128)(2,1)S(1)}, u32[]{:S(2)}, u32[]{:S(2)}) %collective-permute-start.16) | collective-permute-done | bytes 524320 | tf_op jit(solution)/shard_map/ppermute | solution.py:19
  190.7 2.2 fusion.16
  193.3 3.0 collective-permute-start.21
  196.3 1.1 copy.65
  197.4 3.4 %fusion.12 = f32[2,128,2048]{2,1,0:T(8,128)S(1)} fusion(bf16[2,128,1024]{2,1,0:T(8,128)(2,1)S(1)} %bitcast.227, bf16[1,1024,2048]{2,1,0:T(8,128)(2,1)} %param.18), kind=kOutput, calls=%fused_computation.14 | convolution fusion | flops 1073741824 | bytes 6815744 | tf_op jit(solution)/shard_map/dot_general | solution.py:296
  200.8 10.6 %collective-permute-done.19 = bf16[2,1,64,1280]{3,2,1,0:T(8,128)(2,1)S(1)} collective-permute-done((bf16[2,1,64,1280]{3,2,1,0:T(8,128)(2,1)}, bf16[2,1,64,1280]{3,2,1,0:T(8,128)(2,1)S(1)}, u32[]{:S(2)}, u32[]{:S(2)}) %collective-permute-start.19) | collective-permute-done | bytes 327712 | tf_op jit(solution)/shard_map/ppermute | solution.py:19
  211.7 1.9 collective-permute-start.23
  213.6 2.5 collective-permute-start.24
  216.1 1.6 add_bitcast_fusion.3
  217.9 3.3 %collective-permute-done.22.rest_1_ = bf16[256,256]{1,0:T(8,128)(2,1)S(1)} collective-permute-done((bf16[256,256]{1,0:T(8,128)(2,1)S(1)}, bf16[256,256]{1,0:T(8,128)(2,1)S(1)}, u32[]{:S(2)}, u32[]{:S(2)}) %collective-permute-start.22) | collective-permute-done | bytes 131104 | tf_op jit(solution)/shard_map/ppermute | solution.py:23
  221.2 3.6 %collective-permute-done.23.rest_2_ = bf16[256,256]{1,0:T(8,128)(2,1)S(1)} collective-permute-done((bf16[256,256]{1,0:T(8,128)(2,1)S(1)}, bf16[256,256]{1,0:T(8,128)(2,1)S(1)}, u32[]{:S(2)}, u32[]{:S(2)}) %collective-permute-start.23) | collective-permute-done | bytes 131104 | tf_op jit(solution)/shard_map/ppermute | solution.py:23
  224.7 4.4 %shard_map.143 = bf16[256,1024]{1,0:T(8,128)(2,1)S(1)} custom-call(f32[128,1280]{1,0:T(8,128)S(1)} %bitcast.201, f32[128,1280]{1,0:T(8,128)S(1)} %bitcast.205, bf16[128,1280]{1,0:T(8,128)(2,1)S(1)} %bitcast.209, bf16[128,1280]{1,0:T(8,128)(2,1)S(1)} %bitcast.215, f32[256,1]{1,0:T(8,128)S(1)} %squeeze.150.inverse, f32[256,128]{1,0:T(8,128)S(1)} %pad_maximum_fusion.6.cosine, ...), custom_call_target="tpu_custom_call" | custom-call | flops 1073741824 | bytes 2097152 | tf_op jit(solution)/shard_map/pallas_call | solution.py:270
  229.2 2.5 collective-permute-start.28
  231.9 1.3 fusion.19
  233.3 1.3 fusion.8
  234.9 1.1 collective-permute-done.26
  236.4 20.2 %collective-permute-done.29 = bf16[256,1024]{1,0:T(8,128)(2,1)S(1)} collective-permute-done((bf16[256,1024]{1,0:T(8,128)(2,1)S(1)}, bf16[256,1024]{1,0:T(8,128)(2,1)S(1)}, u32[]{:S(2)}, u32[]{:S(2)}) %collective-permute-start.29) | collective-permute-done | bytes 524320 | tf_op jit(solution)/shard_map/ppermute | solution.py:19
  256.7 1.3 fusion.22
  258.1 1.3 constant_dynamic-slice_fusion.1
  259.4 1.6 collective-permute-start.25
  261.6 1.3 fusion.4
  263.4 1.7 collective-permute-start.32
  265.2 10.5 %collective-permute-done.27 = bf16[1,128,2048]{2,1,0:T(8,128)(2,1)S(1)} collective-permute-done((bf16[1,128,2048]{2,1,0:T(8,128)(2,1)S(1)}, bf16[1,128,2048]{2,1,0:T(8,128)(2,1)S(1)}, u32[]{:S(2)}, u32[]{:S(2)}) %collective-permute-start.27) | collective-permute-done | bytes 524320 | tf_op jit(solution)/shard_map/ppermute | solution.py:19
  276.7 1.3 fusion.25
  278.1 1.3 fusion
  279.4 6.8 %collective-permute-done.32 = bf16[1,128,2048]{2,1,0:T(8,128)(2,1)S(1)} collective-permute-done((bf16[1,128,2048]{2,1,0:T(8,128)(2,1)S(1)}, bf16[1,128,2048]{2,1,0:T(8,128)(2,1)S(1)}, u32[]{:S(2)}, u32[]{:S(2)}) %collective-permute-start.32) | collective-permute-done | bytes 524320 | tf_op jit(solution)/shard_map/ppermute | solution.py:19
  288.7 11.8 %collective-permute-done.36 = bf16[1,128,2048]{2,1,0:T(8,128)(2,1)S(1)} collective-permute-done((bf16[1,128,2048]{2,1,0:T(8,128)(2,1)S(1)}, bf16[1,128,2048]{2,1,0:T(8,128)(2,1)S(1)}, u32[]{:S(2)}, u32[]{:S(2)}) %collective-permute-start.36) | collective-permute-done | bytes 524320 | tf_op jit(solution)/shard_map/ppermute | solution.py:19
  300.8 1.6 collective-permute-start.37
  302.6 1.2 reverse_select_fusion.2
  303.8 9.0 %collective-permute-done.37 = bf16[2,64,2048]{2,1,0:T(8,128)(2,1)S(1)} collective-permute-done((bf16[2,64,2048]{2,1,0:T(8,128)(2,1)S(1)}, bf16[2,64,2048]{2,1,0:T(8,128)(2,1)S(1)}, u32[]{:S(2)}, u32[]{:S(2)}) %collective-permute-start.37) | collective-permute-done | bytes 524320 | tf_op jit(solution)/shard_map/ppermute | solution.py:28
  313.2 1.2 reverse_select_fusion
  (148 shorter events, 16.7 us)
Async XLA Ops:
  0.6 3.0 collective-permute-start
  3.6 4.6 %copy-start.8 = (bf16[256,2048]{1,0:T(8,128)(2,1)}, bf16[256,2048]{1,0:T(8,128)(2,1)S(1)}, u32[]{:S(2)}) copy-start(bf16[256,2048]{1,0:T(8,128)(2,1)S(1)} %collective-permute-done) | copy-start | bytes 3145732
  3.6 5.1 %copy-start.5 = (bf16[1,256,2048]{2,1,0:T(8,128)(2,1)S(1)}, bf16[1,256,2048]{2,1,0:T(8,128)(2,1)}, u32[]{:S(2)}) copy-start(bf16[1,256,2048]{2,1,0:T(8,128)(2,1)} %param.13) | copy-start | bytes 3145732
  3.6 10.4 %copy-start.20 = (f32[1,2048]{1,0:T(1,128)S(1)}, f32[1,2048]{1,0:T(1,128)}, u32[]{:S(2)}) copy-start(f32[1,2048]{1,0:T(1,128)} %param.14) | copy-start | bytes 24580
  8.3 10.1 %collective-permute-start.2 = (bf16[256,2048]{1,0:T(8,128)(2,1)}, bf16[256,2048]{1,0:T(8,128)(2,1)}, u32[]{:S(2)}, u32[]{:S(2)}) collective-permute-start(bf16[256,2048]{1,0:T(8,128)(2,1)} %bitcast.12), channel_id=1, source_target_pairs={{0,4},{4,0},{8,12},{12,8},{1,5},{5,1},{9,13},{13,9},{2,6},{6,2},{1... | collective-permute-start | bytes 3145736 | tf_op jit(solution)/shard_map/ppermute | solution.py:19
  8.7 26.3 %collective-permute-start.3 = (bf16[256,2048]{1,0:T(8,128)(2,1)S(1)}, bf16[256,2048]{1,0:T(8,128)(2,1)S(1)}, u32[]{:S(2)}, u32[]{:S(2)}) collective-permute-start(bf16[256,2048]{1,0:T(8,128)(2,1)S(1)} %bitcast.218), channel_id=1, source_target_pairs={{0,8},{4,12},{8,0},{12,4},{1,9},{5,13},{9,1},{13,5},{2,10},{6,14},... | collective-permute-start | bytes 3145736 | tf_op jit(solution)/shard_map/ppermute | solution.py:19
  11.4 16.7 %collective-permute-start.1 = (bf16[2,2,64,1280]{3,2,1,0:T(8,128)(2,1)S(1)}, bf16[2,2,64,1280]{3,2,1,0:T(8,128)(2,1)S(1)}, u32[]{:S(2)}, u32[]{:S(2)}) collective-permute-start(bf16[2,2,64,1280]{3,2,1,0:T(8,128)(2,1)S(1)} %convolution_convert_fusion.3), channel_id=1, source_target_pairs={{0,1},{1,0},{2,3},{3,2},{4,5},{5,4},{6,7},{7,6},{8,9},{9,8},{10,11... | collective-permute-start | bytes 1966088 | tf_op jit(solution)/shard_map/ppermute | solution.py:19
  14.1 4.3 %copy-start.12 = (bf16[1,2048,1024]{2,1,0:T(8,128)(2,1)S(1)}, bf16[1,2048,1024]{2,1,0:T(8,128)(2,1)}, u32[]{:S(2)}) copy-start(bf16[1,2048,1024]{2,1,0:T(8,128)(2,1)} %param.21) | copy-start | bytes 12582916
  14.1 4.3 %copy-start.16 = (bf16[1,2048,128]{2,1,0:T(8,128)(2,1)S(1)}, bf16[1,2048,128]{2,1,0:T(8,128)(2,1)}, u32[]{:S(2)}) copy-start(bf16[1,2048,128]{2,1,0:T(8,128)(2,1)} %param.23) | copy-start | bytes 1572868
  14.1 4.3 %copy-start.18 = (bf16[1,2048,128]{2,1,0:T(8,128)(2,1)S(1)}, bf16[1,2048,128]{2,1,0:T(8,128)(2,1)}, u32[]{:S(2)}) copy-start(bf16[1,2048,128]{2,1,0:T(8,128)(2,1)} %param.22) | copy-start | bytes 1572868
  14.1 4.3 %copy-start.21 = (f32[1,2048]{1,0:T(1,128)S(1)}, f32[1,2048]{1,0:T(1,128)}, u32[]{:S(2)}) copy-start(f32[1,2048]{1,0:T(1,128)} %param.20) | copy-start | bytes 24580
  35.0 36.5 %collective-permute-start.4 = (bf16[256,2048]{1,0:T(8,128)(2,1)S(1)}, bf16[256,2048]{1,0:T(8,128)(2,1)}, u32[]{:S(2)}, u32[]{:S(2)}) collective-permute-start(bf16[256,2048]{1,0:T(8,128)(2,1)S(1)} %collective-permute-done.3), channel_id=1, source_target_pairs={{0,4},{4,0},{8,12},{12,8},{1,5},{5,1},{9,13},{13,9},{2,6},{6,2},{1... | collective-permute-start | bytes 3145736 | tf_op jit(solution)/shard_map/ppermute | solution.py:19
  70.8 14.2 %collective-permute-start.6 = (bf16[2,1,64,1280]{3,2,1,0:T(8,128)(2,1)}, bf16[2,1,64,1280]{3,2,1,0:T(8,128)(2,1)S(1)}, u32[]{:S(2)}, u32[]{:S(2)}) collective-permute-start(bf16[2,1,64,1280]{3,2,1,0:T(8,128)(2,1)} %get-tuple-element.154), channel_id=1, source_target_pairs={{0,2},{1,3},{2,0},{3,1},{4,6},{5,7},{6,4},{7,5},{8,10},{9,11},{10,... | collective-permute-start | bytes 983048 | tf_op jit(solution)/shard_map/ppermute | solution.py:19
  70.9 27.5 %collective-permute-start.9 = (bf16[256,2048]{1,0:T(8,128)(2,1)}, bf16[256,2048]{1,0:T(8,128)(2,1)S(1)}, u32[]{:S(2)}, u32[]{:S(2)}) collective-permute-start(bf16[256,2048]{1,0:T(8,128)(2,1)} %bitcast.12), channel_id=1, source_target_pairs={{0,8},{4,12},{8,0},{12,4},{1,9},{5,13},{9,1},{13,5},{2,10},{6,14},... | collective-permute-start | bytes 3145736 | tf_op jit(solution)/shard_map/ppermute | solution.py:19
  71.5 5.6 %copy-start.11 = (bf16[1,2048,1024]{2,1,0:T(8,128)(2,1)S(1)}, bf16[1,2048,1024]{2,1,0:T(8,128)(2,1)}, u32[]{:S(2)}) copy-start(bf16[1,2048,1024]{2,1,0:T(8,128)(2,1)} %param.15) | copy-start | bytes 12582916
  71.5 5.6 %copy-start.14 = (bf16[1,2048,128]{2,1,0:T(8,128)(2,1)S(1)}, bf16[1,2048,128]{2,1,0:T(8,128)(2,1)}, u32[]{:S(2)}) copy-start(bf16[1,2048,128]{2,1,0:T(8,128)(2,1)} %param.17) | copy-start | bytes 1572868
  71.5 5.6 %copy-start.15 = (bf16[1,2048,128]{2,1,0:T(8,128)(2,1)S(1)}, bf16[1,2048,128]{2,1,0:T(8,128)(2,1)}, u32[]{:S(2)}) copy-start(bf16[1,2048,128]{2,1,0:T(8,128)(2,1)} %param.16) | copy-start | bytes 1572868
  75.9 21.7 %collective-permute-start.5 = (bf16[2,2,64,1280]{3,2,1,0:T(8,128)(2,1)S(1)}, bf16[2,2,64,1280]{3,2,1,0:T(8,128)(2,1)S(1)}, u32[]{:S(2)}, u32[]{:S(2)}) collective-permute-start(bf16[2,2,64,1280]{3,2,1,0:T(8,128)(2,1)S(1)} %convolution_convert_fusion.1), channel_id=1, source_target_pairs={{0,1},{1,0},{2,3},{3,2},{4,5},{5,4},{6,7},{7,6},{8,9},{9,8},{10,11... | collective-permute-start | bytes 1966088 | tf_op jit(solution)/shard_map/ppermute | solution.py:19
  98.4 3.8 %collective-permute-start.10 = (bf16[256,2048]{1,0:T(8,128)(2,1)S(1)}, bf16[256,2048]{1,0:T(8,128)(2,1)}, u32[]{:S(2)}, u32[]{:S(2)}) collective-permute-start(bf16[256,2048]{1,0:T(8,128)(2,1)S(1)} %collective-permute-done.9), channel_id=1, source_target_pairs={{0,4},{4,0},{8,12},{12,8},{1,5},{5,1},{9,13},{13,9},{2,6},{6,2},{1... | collective-permute-start | bytes 3145736 | tf_op jit(solution)/shard_map/ppermute | solution.py:19
  100.2 28.2 %collective-permute-start.7 = (bf16[2,1,64,1280]{3,2,1,0:T(8,128)(2,1)}, bf16[2,1,64,1280]{3,2,1,0:T(8,128)(2,1)S(1)}, u32[]{:S(2)}, u32[]{:S(2)}) collective-permute-start(bf16[2,1,64,1280]{3,2,1,0:T(8,128)(2,1)} %get-tuple-element.152), channel_id=1, source_target_pairs={{0,2},{1,3},{2,0},{3,1},{4,6},{5,7},{6,4},{7,5},{8,10},{9,11},{10,... | collective-permute-start | bytes 983048 | tf_op jit(solution)/shard_map/ppermute | solution.py:19
  100.2 24.4 %collective-permute-start.8 = (bf16[2,2,64,1280]{3,2,1,0:T(8,128)(2,1)}, bf16[2,2,64,1280]{3,2,1,0:T(8,128)(2,1)S(1)}, u32[]{:S(2)}, u32[]{:S(2)}) collective-permute-start(bf16[2,2,64,1280]{3,2,1,0:T(8,128)(2,1)} %convolution_convert_fusion.2), channel_id=1, source_target_pairs={{0,1},{1,0},{2,3},{3,2},{4,5},{5,4},{6,7},{7,6},{8,9},{9,8},{10,11... | collective-permute-start | bytes 1966088 | tf_op jit(solution)/shard_map/ppermute | solution.py:19
  102.3 6.4 %copy-start.13 = (bf16[1,2048,1024]{2,1,0:T(8,128)(2,1)S(1)}, bf16[1,2048,1024]{2,1,0:T(8,128)(2,1)}, u32[]{:S(2)}) copy-start(bf16[1,2048,1024]{2,1,0:T(8,128)(2,1)} %param.21) | copy-start | bytes 12582916
  102.3 6.4 %copy-start.17 = (bf16[1,2048,128]{2,1,0:T(8,128)(2,1)S(1)}, bf16[1,2048,128]{2,1,0:T(8,128)(2,1)}, u32[]{:S(2)}) copy-start(bf16[1,2048,128]{2,1,0:T(8,128)(2,1)} %param.23) | copy-start | bytes 1572868
  102.3 6.4 %copy-start.19 = (bf16[1,2048,128]{2,1,0:T(8,128)(2,1)S(1)}, bf16[1,2048,128]{2,1,0:T(8,128)(2,1)}, u32[]{:S(2)}) copy-start(bf16[1,2048,128]{2,1,0:T(8,128)(2,1)} %param.22) | copy-start | bytes 1572868
  108.6 16.0 %copy-start.7 = (f32[2,2,64,1280]{3,2,1,0:T(8,128)S(1)}, f32[2,2,64,1280]{3,2,1,0:T(8,128)}, u32[]{:S(2)}) copy-start(f32[2,2,64,1280]{3,2,1,0:T(8,128)} %fusion.33) | copy-start | bytes 3932164
  125.5 17.6 %collective-permute-start.14 = (bf16[2,1,64,1280]{3,2,1,0:T(8,128)(2,1)}, bf16[2,1,64,1280]{3,2,1,0:T(8,128)(2,1)S(1)}, u32[]{:S(2)}, u32[]{:S(2)}) collective-permute-start(bf16[2,1,64,1280]{3,2,1,0:T(8,128)(2,1)} %get-tuple-element.151), channel_id=1, source_target_pairs={{0,2},{1,3},{2,0},{3,1},{4,6},{5,7},{6,4},{7,5},{8,10},{9,11},{10,... | collective-permute-start | bytes 983048 | tf_op jit(solution)/shard_map/ppermute | solution.py:19
  126.0 41.4 %collective-permute-start.17 = (bf16[2,2,64,1280]{3,2,1,0:T(8,128)(2,1)}, bf16[2,2,64,1280]{3,2,1,0:T(8,128)(2,1)}, u32[]{:S(2)}, u32[]{:S(2)}) collective-permute-start(bf16[2,2,64,1280]{3,2,1,0:T(8,128)(2,1)} %convolution_convert_fusion), channel_id=1, source_target_pairs={{0,1},{1,0},{2,3},{3,2},{4,5},{5,4},{6,7},{7,6},{8,9},{9,8},{10,11... | collective-permute-start | bytes 1966088 | tf_op jit(solution)/shard_map/ppermute | solution.py:19
  128.7 28.1 %collective-permute-start.11 = (bf16[256,256]{1,0:T(8,128)(2,1)S(1)}, bf16[256,256]{1,0:T(8,128)(2,1)}, u32[]{:S(2)}, u32[]{:S(2)}) collective-permute-start(bf16[256,256]{1,0:T(8,128)(2,1)S(1)} %shard_map.140.rest_0_), channel_id=1, source_target_pairs={{0,1},{1,0},{2,3},{3,2},{4,5},{5,4},{6,7},{7,6},{8,9},{9,8},{10,11... | collective-permute-start | bytes 393224 | tf_op jit(solution)/shard_map/ppermute | solution.py:23
  128.8 28.0 %collective-permute-start.12 = (bf16[256,256]{1,0:T(8,128)(2,1)S(1)}, bf16[256,256]{1,0:T(8,128)(2,1)}, u32[]{:S(2)}, u32[]{:S(2)}) collective-permute-start(bf16[256,256]{1,0:T(8,128)(2,1)S(1)} %shard_map.140.rest_0_), channel_id=1, source_target_pairs={{0,2},{1,3},{2,0},{3,1},{4,6},{5,7},{6,4},{7,5},{8,10},{9,11},{10,... | collective-permute-start | bytes 393224 | tf_op jit(solution)/shard_map/ppermute | solution.py:23
  130.8 27.7 %collective-permute-start.13 = (bf16[256,256]{1,0:T(8,128)(2,1)S(1)}, bf16[256,256]{1,0:T(8,128)(2,1)}, u32[]{:S(2)}, u32[]{:S(2)}) collective-permute-start(bf16[256,256]{1,0:T(8,128)(2,1)S(1)} %shard_map.140.rest_0_), channel_id=1, source_target_pairs={{0,3},{1,2},{2,1},{3,0},{4,7},{5,6},{6,5},{7,4},{8,11},{9,10},{10,... | collective-permute-start | bytes 393224 | tf_op jit(solution)/shard_map/ppermute | solution.py:23
  158.5 0.9 copy-start
  159.4 31.3 %copy-start.2 = (bf16[1,1024,2048]{2,1,0:T(8,128)(2,1)S(1)}, bf16[1,1024,2048]{2,1,0:T(8,128)(2,1)}, u32[]{:S(2)}) copy-start(bf16[1,1024,2048]{2,1,0:T(8,128)(2,1)} %param.18) | copy-start | bytes 12582916
  165.1 23.9 %collective-permute-start.16 = (bf16[256,1024]{1,0:T(8,128)(2,1)S(1)}, bf16[256,1024]{1,0:T(8,128)(2,1)S(1)}, u32[]{:S(2)}, u32[]{:S(2)}) collective-permute-start(bf16[256,1024]{1,0:T(8,128)(2,1)S(1)} %shard_map.141), channel_id=1, source_target_pairs={{0,2},{1,3},{2,0},{3,1},{4,6},{5,7},{6,4},{7,5},{8,10},{9,11},{10,... | collective-permute-start | bytes 1572872 | tf_op jit(solution)/shard_map/ppermute | solution.py:19
  165.2 24.2 %collective-permute-start.15 = (bf16[256,1024]{1,0:T(8,128)(2,1)S(1)}, bf16[256,1024]{1,0:T(8,128)(2,1)S(1)}, u32[]{:S(2)}, u32[]{:S(2)}) collective-permute-start(bf16[256,1024]{1,0:T(8,128)(2,1)S(1)} %shard_map.141), channel_id=1, source_target_pairs={{0,1},{1,0},{2,3},{3,2},{4,5},{5,4},{6,7},{7,6},{8,9},{9,8},{10,11... | collective-permute-start | bytes 1572872 | tf_op jit(solution)/shard_map/ppermute | solution.py:19
  189.0 0.8 copy-start.9
  190.7 2.4 copy-start.6
  192.9 23.2 %collective-permute-start.18 = (bf16[2,128,2048]{2,1,0:T(8,128)(2,1)}, bf16[2,128,2048]{2,1,0:T(8,128)(2,1)}, u32[]{:S(2)}, u32[]{:S(2)}) collective-permute-start(bf16[2,128,2048]{2,1,0:T(8,128)(2,1)} %fusion.16), channel_id=1, source_target_pairs={{0,4},{4,0},{8,12},{12,8},{1,5},{5,1},{9,13},{13,9},{2,6},{6,2},{1... | collective-permute-start | bytes 3145736 | tf_op jit(solution)/shard_map/ppermute | solution.py:19
  193.2 18.3 %collective-permute-start.19 = (bf16[2,1,64,1280]{3,2,1,0:T(8,128)(2,1)}, bf16[2,1,64,1280]{3,2,1,0:T(8,128)(2,1)S(1)}, u32[]{:S(2)}, u32[]{:S(2)}) collective-permute-start(bf16[2,1,64,1280]{3,2,1,0:T(8,128)(2,1)} %get-tuple-element.149), channel_id=1, source_target_pairs={{0,2},{1,3},{2,0},{3,1},{4,6},{5,7},{6,4},{7,5},{8,10},{9,11},{10,... | collective-permute-start | bytes 983048 | tf_op jit(solution)/shard_map/ppermute | solution.py:19
  193.3 38.5 %collective-permute-start.21 = (bf16[256,1024]{1,0:T(8,128)(2,1)}, bf16[256,1024]{1,0:T(8,128)(2,1)S(1)}, u32[]{:S(2)}, u32[]{:S(2)}) collective-permute-start(bf16[256,1024]{1,0:T(8,128)(2,1)} %copy-done.9), channel_id=1, source_target_pairs={{0,1},{1,0},{2,3},{3,2},{4,5},{5,4},{6,7},{7,6},{8,9},{9,8},{10,11... | collective-permute-start | bytes 1572872 | tf_op jit(solution)/shard_map/ppermute | solution.py:19
  211.5 13.3 %copy-start.1 = (f32[256,1]{1,0:T(8,128)S(1)}, f32[256,1]{1,0:T(8,128)}, u32[]{:S(2)}) copy-start(f32[256,1]{1,0:T(8,128)} %convert_element_type.371.q_pos) | copy-start | bytes 3076
  211.7 9.5 %collective-permute-start.22 = (bf16[256,256]{1,0:T(8,128)(2,1)S(1)}, bf16[256,256]{1,0:T(8,128)(2,1)S(1)}, u32[]{:S(2)}, u32[]{:S(2)}) collective-permute-start(bf16[256,256]{1,0:T(8,128)(2,1)S(1)} %shard_map.142.rest_0_), channel_id=1, source_target_pairs={{0,1},{1,0},{2,3},{3,2},{4,5},{5,4},{6,7},{7,6},{8,9},{9,8},{10,11... | collective-permute-start | bytes 393224 | tf_op jit(solution)/shard_map/ppermute | solution.py:23
  211.7 13.0 %collective-permute-start.23 = (bf16[256,256]{1,0:T(8,128)(2,1)S(1)}, bf16[256,256]{1,0:T(8,128)(2,1)S(1)}, u32[]{:S(2)}, u32[]{:S(2)}) collective-permute-start(bf16[256,256]{1,0:T(8,128)(2,1)S(1)} %shard_map.142.rest_0_), channel_id=1, source_target_pairs={{0,2},{1,3},{2,0},{3,1},{4,6},{5,7},{6,4},{7,5},{8,10},{9,11},{10,... | collective-permute-start | bytes 393224 | tf_op jit(solution)/shard_map/ppermute | solution.py:23
  213.6 11.1 %collective-permute-start.24 = (bf16[256,256]{1,0:T(8,128)(2,1)S(1)}, bf16[256,256]{1,0:T(8,128)(2,1)S(1)}, u32[]{:S(2)}, u32[]{:S(2)}) collective-permute-start(bf16[256,256]{1,0:T(8,128)(2,1)S(1)} %shard_map.142.rest_0_), channel_id=1, source_target_pairs={{0,3},{1,2},{2,1},{3,0},{4,7},{5,6},{6,5},{7,4},{8,11},{9,10},{10,... | collective-permute-start | bytes 393224 | tf_op jit(solution)/shard_map/ppermute | solution.py:23
  217.7 14.1 %copy-start.10 = (bf16[256,1024]{1,0:T(8,128)(2,1)S(1)}, bf16[256,1024]{1,0:T(8,128)(2,1)}, u32[]{:S(2)}) copy-start(bf16[256,1024]{1,0:T(8,128)(2,1)} %copy-done.9) | copy-start | bytes 1572868
  217.8 14.1 %copy-start.3 = (bf16[1,1024,2048]{2,1,0:T(8,128)(2,1)S(1)}, bf16[1,1024,2048]{2,1,0:T(8,128)(2,1)}, u32[]{:S(2)}) copy-start(bf16[1,1024,2048]{2,1,0:T(8,128)(2,1)} %param.18) | copy-start | bytes 12582916
  217.8 16.8 %collective-permute-start.20 = (bf16[1,128,2048]{2,1,0:T(8,128)(2,1)S(1)}, bf16[1,128,2048]{2,1,0:T(8,128)(2,1)S(1)}, u32[]{:S(2)}, u32[]{:S(2)}) collective-permute-start(bf16[1,128,2048]{2,1,0:T(8,128)(2,1)S(1)} %fusion.76), channel_id=1, source_target_pairs={{0,8},{4,12},{8,0},{12,4},{1,9},{5,13},{9,1},{13,5},{2,10},{6,14},... | collective-permute-start | bytes 1572872 | tf_op jit(solution)/shard_map/ppermute | solution.py:19
  229.2 27.4 %collective-permute-start.28 = (bf16[256,1024]{1,0:T(8,128)(2,1)S(1)}, bf16[256,1024]{1,0:T(8,128)(2,1)S(1)}, u32[]{:S(2)}, u32[]{:S(2)}) collective-permute-start(bf16[256,1024]{1,0:T(8,128)(2,1)S(1)} %shard_map.143), channel_id=1, source_target_pairs={{0,1},{1,0},{2,3},{3,2},{4,5},{5,4},{6,7},{7,6},{8,9},{9,8},{10,11... | collective-permute-start | bytes 1572872 | tf_op jit(solution)/shard_map/ppermute | solution.py:19
  231.7 24.9 %collective-permute-start.29 = (bf16[256,1024]{1,0:T(8,128)(2,1)S(1)}, bf16[256,1024]{1,0:T(8,128)(2,1)S(1)}, u32[]{:S(2)}, u32[]{:S(2)}) collective-permute-start(bf16[256,1024]{1,0:T(8,128)(2,1)S(1)} %shard_map.143), channel_id=1, source_target_pairs={{0,2},{1,3},{2,0},{3,1},{4,6},{5,7},{6,4},{7,5},{8,10},{9,11},{10,... | collective-permute-start | bytes 1572872 | tf_op jit(solution)/shard_map/ppermute | solution.py:19
  233.2 2.7 collective-permute-start.26
  234.9 21.9 %copy-start.4 = (bf16[1,1024,2048]{2,1,0:T(8,128)(2,1)S(1)}, bf16[1,1024,2048]{2,1,0:T(8,128)(2,1)}, u32[]{:S(2)}) copy-start(bf16[1,1024,2048]{2,1,0:T(8,128)(2,1)} %param.24) | copy-start | bytes 12582916
  258.0 5.0 %collective-permute-start.30 = (bf16[2,128,2048]{2,1,0:T(8,128)(2,1)S(1)}, bf16[2,128,2048]{2,1,0:T(8,128)(2,1)S(1)}, u32[]{:S(2)}, u32[]{:S(2)}) collective-permute-start(bf16[2,128,2048]{2,1,0:T(8,128)(2,1)S(1)} %fusion.22), channel_id=1, source_target_pairs={{0,4},{4,0},{8,12},{12,8},{1,5},{5,1},{9,13},{13,9},{2,6},{6,2},{1... | collective-permute-start | bytes 3145736 | tf_op jit(solution)/shard_map/ppermute | solution.py:19
  259.4 28.5 %collective-permute-start.25 = (bf16[2,64,2048]{2,1,0:T(8,128)(2,1)S(1)}, bf16[2,64,2048]{2,1,0:T(8,128)(2,1)S(1)}, u32[]{:S(2)}, u32[]{:S(2)}) collective-permute-start(bf16[2,64,2048]{2,1,0:T(8,128)(2,1)S(1)} %add_convert_fusion.3), channel_id=1, source_target_pairs={{0,16},{16,0},{1,17},{17,1},{2,18},{18,2},{3,19},{19,3},{4,20},{20... | collective-permute-start | bytes 1572872 | tf_op jit(solution)/shard_map/ppermute | solution.py:28
  261.0 14.8 %collective-permute-start.27 = (bf16[1,128,2048]{2,1,0:T(8,128)(2,1)S(1)}, bf16[1,128,2048]{2,1,0:T(8,128)(2,1)S(1)}, u32[]{:S(2)}, u32[]{:S(2)}) collective-permute-start(bf16[1,128,2048]{2,1,0:T(8,128)(2,1)S(1)} %fusion.77), channel_id=1, source_target_pairs={{0,8},{4,12},{8,0},{12,4},{1,9},{5,13},{9,1},{13,5},{2,10},{6,14},... | collective-permute-start | bytes 1572872 | tf_op jit(solution)/shard_map/ppermute | solution.py:19
  261.0 15.6 %collective-permute-start.33 = (bf16[256,1024]{1,0:T(8,128)(2,1)S(1)}, bf16[256,1024]{1,0:T(8,128)(2,1)S(1)}, u32[]{:S(2)}, u32[]{:S(2)}) collective-permute-start(bf16[256,1024]{1,0:T(8,128)(2,1)S(1)} %collective-permute-done.29), channel_id=1, source_target_pairs={{0,1},{1,0},{2,3},{3,2},{4,5},{5,4},{6,7},{7,6},{8,9},{9,8},{10,11... | collective-permute-start | bytes 1572872 | tf_op jit(solution)/shard_map/ppermute | solution.py:19
  263.4 22.8 %collective-permute-start.32 = (bf16[1,128,2048]{2,1,0:T(8,128)(2,1)S(1)}, bf16[1,128,2048]{2,1,0:T(8,128)(2,1)S(1)}, u32[]{:S(2)}, u32[]{:S(2)}) collective-permute-start(bf16[1,128,2048]{2,1,0:T(8,128)(2,1)S(1)} %fusion.78), channel_id=1, source_target_pairs={{0,8},{4,12},{8,0},{12,4},{1,9},{5,13},{9,1},{13,5},{2,10},{6,14},... | collective-permute-start | bytes 1572872 | tf_op jit(solution)/shard_map/ppermute | solution.py:19
  275.9 12.5 %collective-permute-start.31 = (bf16[2,64,2048]{2,1,0:T(8,128)(2,1)S(1)}, bf16[2,64,2048]{2,1,0:T(8,128)(2,1)S(1)}, u32[]{:S(2)}, u32[]{:S(2)}) collective-permute-start(bf16[2,64,2048]{2,1,0:T(8,128)(2,1)S(1)} %add_convert_fusion.2), channel_id=1, source_target_pairs={{0,16},{16,0},{1,17},{17,1},{2,18},{18,2},{3,19},{19,3},{4,20},{20... | collective-permute-start | bytes 1572872 | tf_op jit(solution)/shard_map/ppermute | solution.py:28
  278.0 9.1 %collective-permute-start.35 = (bf16[2,128,2048]{2,1,0:T(8,128)(2,1)S(1)}, bf16[2,128,2048]{2,1,0:T(8,128)(2,1)S(1)}, u32[]{:S(2)}, u32[]{:S(2)}) collective-permute-start(bf16[2,128,2048]{2,1,0:T(8,128)(2,1)S(1)} %fusion.25), channel_id=1, source_target_pairs={{0,4},{4,0},{8,12},{12,8},{1,5},{5,1},{9,13},{13,9},{2,6},{6,2},{1... | collective-permute-start | bytes 3145736 | tf_op jit(solution)/shard_map/ppermute | solution.py:19
  286.5 17.3 %collective-permute-start.34 = (bf16[2,64,2048]{2,1,0:T(8,128)(2,1)S(1)}, bf16[2,64,2048]{2,1,0:T(8,128)(2,1)S(1)}, u32[]{:S(2)}, u32[]{:S(2)}) collective-permute-start(bf16[2,64,2048]{2,1,0:T(8,128)(2,1)S(1)} %add_convert_fusion.1), channel_id=1, source_target_pairs={{0,16},{16,0},{1,17},{17,1},{2,18},{18,2},{3,19},{19,3},{4,20},{20... | collective-permute-start | bytes 1572872 | tf_op jit(solution)/shard_map/ppermute | solution.py:28
  287.5 13.0 %collective-permute-start.36 = (bf16[1,128,2048]{2,1,0:T(8,128)(2,1)S(1)}, bf16[1,128,2048]{2,1,0:T(8,128)(2,1)S(1)}, u32[]{:S(2)}, u32[]{:S(2)}) collective-permute-start(bf16[1,128,2048]{2,1,0:T(8,128)(2,1)S(1)} %fusion.79), channel_id=1, source_target_pairs={{0,8},{4,12},{8,0},{12,4},{1,9},{5,13},{9,1},{13,5},{2,10},{6,14},... | collective-permute-start | bytes 1572872 | tf_op jit(solution)/shard_map/ppermute | solution.py:19
  300.8 12.1 %collective-permute-start.37 = (bf16[2,64,2048]{2,1,0:T(8,128)(2,1)S(1)}, bf16[2,64,2048]{2,1,0:T(8,128)(2,1)S(1)}, u32[]{:S(2)}, u32[]{:S(2)}) collective-permute-start(bf16[2,64,2048]{2,1,0:T(8,128)(2,1)S(1)} %add_convert_fusion), channel_id=1, source_target_pairs={{0,16},{16,0},{1,17},{17,1},{2,18},{18,2},{3,19},{19,3},{4,20},{20... | collective-permute-start | bytes 1572872 | tf_op jit(solution)/shard_map/ppermute | solution.py:28
